TPU v7x, 512 devices: a whole 4x8x8 slice. The times are simulated.
512 devices in a mesh: row: 16 (over x, y_lo, core), col: 32 (over z, y_hi).
Axes of the slice: x: 4, y: 8 (y_hi: 4, y_lo: 2; y = y_hi * 2 + y_lo), z: 8, core: 2. Of those that a mesh axis runs over, the one named last changes fastest.
Arguments:
- eigvecs: float32 [4096, 4096], P('row', 'col'), may hold values from -6 to 6
- offsets: int32 [1], replicated, may hold values from 0 to 127
- plan: int32 [1, 30], replicated, may hold values from 0 to 31
- refl_v: float32 [32, 255, 128], P('col')
- refl_t: float32 [32, 128, 128], P('col'), as said below
Outputs:
- updated: float32 [4096, 4096], P('row', 'col')
Inputs may be any that keep to these rules, and one draw needn't show every extreme that they name: For each bank entry, I - refl_v refl_t refl_v^T is orthogonal up to rounding.
All inputs are finite; a program needn't handle non-finite values.
Results may differ from a plain program's by a relative error of at most 0.00015.
Values sent between devices are 32-bit elements; how exact they have to be, the bound alone decides.
A program may use at most 64 MiB of HBM per device.

v0:
```python
import jax
import jax.numpy as jnp
from jax import lax
from jax.sharding import PartitionSpec as P

HIGHEST = lax.Precision.HIGHEST


def from_root(value, axis, root):
    mine = lax.axis_index(axis) == root
    return lax.psum(jnp.where(mine, value, jnp.zeros_like(value)), axis)


def from_behind(value, axis, by):
    devices = lax.axis_size(axis)
    pairs = [(i, i + by) for i in range(devices) if 0 <= i + by < devices]
    return lax.ppermute(value, axis, pairs)


def apply_one(extended, row_start, vectors, factor, weight):
    span_rows = vectors.shape[0]
    block_rows = lax.dynamic_slice_in_dim(extended, row_start, span_rows, 0)
    inner_prod = jnp.dot(vectors.T, block_rows, precision=HIGHEST)
    scaled = jnp.dot(factor, inner_prod, precision=HIGHEST)
    block_rows = block_rows - weight * jnp.dot(vectors, scaled, precision=HIGHEST)
    return lax.dynamic_update_slice_in_dim(extended, block_rows, row_start, 0)


def on_device(eigvecs, offsets, plan, refl_v, refl_t):
    rows_dev = eigvecs.shape[0]
    band = refl_v.shape[2]
    span_rows = refl_v.shape[1]
    per_device = rows_dev // band
    bank_dev = refl_v.shape[0]
    row_count = lax.axis_size("row")
    my_row = lax.axis_index("row")
    sweep_count = offsets.shape[0]
    block_total = row_count * per_device - 2
    head_count = 2 * band
    padded_ids = jnp.pad(plan, ((0, 0), (0, 2)))
    my_ids = lax.dynamic_slice_in_dim(padded_ids, my_row * per_device, per_device, 1).reshape(-1)
    needed = sweep_count * per_device

    def fetch_block(index, stored):
        block_id = my_ids[index]
        owner_col = block_id // bank_dev
        owner_slot = block_id % bank_dev
        got_v, got_t = (
            from_root(refl_v[owner_slot], "col", owner_col),
            from_root(refl_t[owner_slot], "col", owner_col),
        )
        return (stored[0].at[index].set(got_v), stored[1].at[index].set(got_t))

    empty = (
        jnp.zeros((needed, span_rows, band), jnp.float32),
        jnp.zeros((needed, band, band), jnp.float32),
    )
    local_v, local_t = lax.fori_loop(0, needed, fetch_block, empty)
    tick_count = 2 * sweep_count - 2 + row_count

    def run_tick(tick, matrix):
        fetched = from_behind(matrix, "row", -1)
        lag = tick - my_row
        active = (lag >= 0) & (lag % 2 == 0) & (lag < 2 * sweep_count)
        sweep = jnp.clip(lag // 2, 0, sweep_count - 1)
        first_row = offsets[sweep]

        def process(current):
            extended = jnp.concatenate([current, fetched], 0)

            def apply_block(index, extended):
                row_start = first_row + index * band
                slot = sweep * per_device + index
                is_valid = (my_row * per_device + index < block_total).astype(jnp.float32)
                return apply_one(extended, row_start, local_v[slot], local_t[slot], is_valid)

            return lax.fori_loop(0, per_device, apply_block, extended)

        def unchanged(current):
            return jnp.concatenate([current, fetched], 0)

        extended = lax.cond(active, process, unchanged, matrix)
        returned = from_behind(extended[rows_dev:], "row", 1)
        sender_lag = lag + 1
        sender_live = (
            (my_row >= 1)
            & (sender_lag >= 0)
            & (sender_lag % 2 == 0)
            & (sender_lag < 2 * sweep_count)
        )
        matrix = extended[:rows_dev]
        new_head = jnp.where(sender_live, returned, matrix)
        return matrix.at[:head_count].set(new_head)

    return lax.fori_loop(0, tick_count, run_tick, eigvecs)


def solution(mesh):
    in_specs = (P("row", "col"), P(), P(), P("col", None, None), P("col", None, None))
    out_specs = P("row", "col")
    return jax.shard_map(
        on_device, mesh=mesh, in_specs=in_specs, out_specs=out_specs, check_vma=False
    )
```

profile of v0, /device:TPU:7, one launch (start us, length us, event | category | flops | bytes accessed | tf_op | source)
XLA Modules:
  0.0 990.6 jit_solution(11573870405648408309)
XLA Ops:
  8.3 603.7 %while.62 = (s32[]{:T(128)}, f32[2,255,128]{2,1,0:T(8,128)S(1)}, f32[2,128,128]{2,1,0:T(8,128)S(1)}, s32[2]{0:T(128)S(1)}, f32[1,255,128]{2,1,0:T(8,128)S(1)}, /...) while((s32[]{:T(128)}, f32[2,255,128]{2,1,0:T(8,128)S(1)}, ...), condition=%wide.region_4.5_spmd, body=%wide.region_0.4_spmd.sunk | while | flops 147094 | bytes 2421499 | solution.py:58
  11.6 291.2 %all-reduce.6.cloned.1.call-done = (f32[1,255,128]{2,1,0:T(8,128)}, f32[1,128,128]{2,1,0:T(8,128)}) async-done(((f32[1,255,128]{2,1,0:T(8,128)}, f32[1,128,128]{2,1,0:T(8,128)}), (f32[1,255,128]{2,1,0:T(8,128)}, f32[1,128,128]{2,1,0:T(8,128)})) %all-reduce.6.cloned.1.call-update) | async-done | bytes 196112 | tf_op jit(solution)/shard_map/while/body/eval_jaxpr/psum | solution.py:11
  302.8 1.5 select_dynamic-update-slice_fusion.4
  308.3 301.6 %all-reduce.6.cloned.1.call-done = (f32[1,255,128]{2,1,0:T(8,128)}, f32[1,128,128]{2,1,0:T(8,128)}) async-done(((f32[1,255,128]{2,1,0:T(8,128)}, f32[1,128,128]{2,1,0:T(8,128)}), (f32[1,255,128]{2,1,0:T(8,128)}, f32[1,128,128]{2,1,0:T(8,128)})) %all-reduce.6.cloned.1.call-update) | async-done | bytes 196112 | tf_op jit(solution)/shard_map/while/body/eval_jaxpr/psum | solution.py:11
  609.9 1.5 select_dynamic-update-slice_fusion.4
  612.1 371.0 %while.63 = (s32[]{:T(128)}, f32[256,128]{1,0:T(8,128)S(1)}, s32[]{:T(128)}, pred[]{:T(512)}, s32[1]{0:T(128)}, /*index=5*/f32[2,255,128]{2,1,0:T(8,128)S(1)}, f...) while((s32[]{:T(128)}, f32[256,128]{1,0:T(8,128)S(1)}, s32[]{:T(128)}, pred[]{:T(512)}, ...), condition=%wide.region_10.11_spmd, body=%wide.region_5.10_spmd.sunk | while | flops 125599528 | bytes 3472517 | solution.py:95
  612.1 23.0 %collective-permute-start = (f32[256,128]{1,0:T(8,128)S(1)}, f32[256,128]{1,0:T(8,128)S(1)}, u32[]{:S(2)}, u32[]{:S(2)}) collective-permute-start(f32[256,128]{1,0:T(8,128)S(1)} %get-tuple-element.970), channel_id=1, source_target_pairs={{32,0},{64,32},{96,64},{128,96},{160,128},{192,160},{224,192},{256... | collective-permute-start | bytes 393224 | tf_op jit(solution)/shard_map/while/body/eval_jaxpr/ppermute | solution.py:17
  635.2 2.8 collective-permute-done
  639.6 1.9 collective-permute-start.1
  641.6 1.9 collective-permute-done.1
  644.4 5.0 collective-permute-start
  649.5 1.9 collective-permute-done
  653.0 1.9 collective-permute-start.1
  655.0 1.9 collective-permute-done.1
  657.8 5.9 collective-permute-start
  666.5 1.9 collective-permute-start.1
  668.4 2.2 collective-permute-done.1
  671.6 6.5 collective-permute-start
  680.7 1.9 collective-permute-start.1
  682.7 2.3 collective-permute-done.1
  686.0 6.5 collective-permute-start
  695.0 1.9 collective-permute-start.1
  697.0 2.3 collective-permute-done.1
  700.3 6.5 collective-permute-start
  709.4 1.9 collective-permute-start.1
  711.3 2.3 collective-permute-done.1
  714.6 6.5 collective-permute-start
  723.7 1.9 collective-permute-start.1
  725.7 2.3 collective-permute-done.1
  728.9 6.5 collective-permute-start
  738.0 1.9 collective-permute-start.1
  740.0 9.2 collective-permute-done.1
  750.2 17.6 %collective-permute-start = (f32[256,128]{1,0:T(8,128)S(1)}, f32[256,128]{1,0:T(8,128)S(1)}, u32[]{:S(2)}, u32[]{:S(2)}) collective-permute-start(f32[256,128]{1,0:T(8,128)S(1)} %get-tuple-element.970), channel_id=1, source_target_pairs={{32,0},{64,32},{96,64},{128,96},{160,128},{192,160},{224,192},{256... | collective-permute-start | bytes 393224 | tf_op jit(solution)/shard_map/while/body/eval_jaxpr/ppermute | solution.py:17
  770.4 1.9 collective-permute-start.1
  772.4 11.3 %collective-permute-done.1 = f32[256,128]{1,0:T(8,128)S(1)} collective-permute-done((f32[256,128]{1,0:T(8,128)S(1)}, f32[256,128]{1,0:T(8,128)S(1)}, u32[]{:S(2)}, u32[]{:S(2)}) %collective-permute-start.1) | collective-permute-done | bytes 131104 | tf_op jit(solution)/shard_map/while/body/eval_jaxpr/ppermute | solution.py:17
  784.6 17.5 %collective-permute-start = (f32[256,128]{1,0:T(8,128)S(1)}, f32[256,128]{1,0:T(8,128)S(1)}, u32[]{:S(2)}, u32[]{:S(2)}) collective-permute-start(f32[256,128]{1,0:T(8,128)S(1)} %get-tuple-element.970), channel_id=1, source_target_pairs={{32,0},{64,32},{96,64},{128,96},{160,128},{192,160},{224,192},{256... | collective-permute-start | bytes 393224 | tf_op jit(solution)/shard_map/while/body/eval_jaxpr/ppermute | solution.py:17
  804.7 1.9 collective-permute-start.1
  806.6 11.6 %collective-permute-done.1 = f32[256,128]{1,0:T(8,128)S(1)} collective-permute-done((f32[256,128]{1,0:T(8,128)S(1)}, f32[256,128]{1,0:T(8,128)S(1)}, u32[]{:S(2)}, u32[]{:S(2)}) %collective-permute-start.1) | collective-permute-done | bytes 131104 | tf_op jit(solution)/shard_map/while/body/eval_jaxpr/ppermute | solution.py:17
  819.1 17.1 %collective-permute-start = (f32[256,128]{1,0:T(8,128)S(1)}, f32[256,128]{1,0:T(8,128)S(1)}, u32[]{:S(2)}, u32[]{:S(2)}) collective-permute-start(f32[256,128]{1,0:T(8,128)S(1)} %get-tuple-element.970), channel_id=1, source_target_pairs={{32,0},{64,32},{96,64},{128,96},{160,128},{192,160},{224,192},{256... | collective-permute-start | bytes 393224 | tf_op jit(solution)/shard_map/while/body/eval_jaxpr/ppermute | solution.py:17
  838.8 1.9 collective-permute-start.1
  840.8 11.8 %collective-permute-done.1 = f32[256,128]{1,0:T(8,128)S(1)} collective-permute-done((f32[256,128]{1,0:T(8,128)S(1)}, f32[256,128]{1,0:T(8,128)S(1)}, u32[]{:S(2)}, u32[]{:S(2)}) %collective-permute-start.1) | collective-permute-done | bytes 131104 | tf_op jit(solution)/shard_map/while/body/eval_jaxpr/ppermute | solution.py:17
  853.5 16.9 %collective-permute-start = (f32[256,128]{1,0:T(8,128)S(1)}, f32[256,128]{1,0:T(8,128)S(1)}, u32[]{:S(2)}, u32[]{:S(2)}) collective-permute-start(f32[256,128]{1,0:T(8,128)S(1)} %get-tuple-element.970), channel_id=1, source_target_pairs={{32,0},{64,32},{96,64},{128,96},{160,128},{192,160},{224,192},{256... | collective-permute-start | bytes 393224 | tf_op jit(solution)/shard_map/while/body/eval_jaxpr/ppermute | solution.py:17
  873.1 1.9 collective-permute-start.1
  875.0 12.1 %collective-permute-done.1 = f32[256,128]{1,0:T(8,128)S(1)} collective-permute-done((f32[256,128]{1,0:T(8,128)S(1)}, f32[256,128]{1,0:T(8,128)S(1)}, u32[]{:S(2)}, u32[]{:S(2)}) %collective-permute-start.1) | collective-permute-done | bytes 131104 | tf_op jit(solution)/shard_map/while/body/eval_jaxpr/ppermute | solution.py:17
  888.1 16.5 %collective-permute-start = (f32[256,128]{1,0:T(8,128)S(1)}, f32[256,128]{1,0:T(8,128)S(1)}, u32[]{:S(2)}, u32[]{:S(2)}) collective-permute-start(f32[256,128]{1,0:T(8,128)S(1)} %get-tuple-element.970), channel_id=1, source_target_pairs={{32,0},{64,32},{96,64},{128,96},{160,128},{192,160},{224,192},{256... | collective-permute-start | bytes 393224 | tf_op jit(solution)/shard_map/while/body/eval_jaxpr/ppermute | solution.py:17
  907.2 1.9 collective-permute-start.1
  909.2 12.4 %collective-permute-done.1 = f32[256,128]{1,0:T(8,128)S(1)} collective-permute-done((f32[256,128]{1,0:T(8,128)S(1)}, f32[256,128]{1,0:T(8,128)S(1)}, u32[]{:S(2)}, u32[]{:S(2)}) %collective-permute-start.1) | collective-permute-done | bytes 131104 | tf_op jit(solution)/shard_map/while/body/eval_jaxpr/ppermute | solution.py:17
  922.5 6.3 collective-permute-start
  929.8 10.8 %conditional.2 = (f32[512,128]{1,0:T(8,128)}) conditional(s32[]{:T(128)} %convert_element_type.21, (f32[256,128]{1,0:T(8,128)S(1)}, f32[256,128]{1,0:T(8,128)S(1)}) %tuple.149, (f32[256,128]{1,0:T(8,128)S(1)}, f32[256,128]{1,0:T(8,128)S(1)}, s32[1]{0:T(128)}, s32[]{:T(128)}, s32[]{:T(128)}, /*index=5*/s32[]{:T(128)}, pred[]{:T(512)}, ...), branch_computations={%region_6.6_spmd, %region_7.9_spmd} | conditional | flops 125566744 | bytes 1767995 | solution.py:82
  930.5 10.0 %while.61 = (s32[]{:T(128)}, f32[512,128]{1,0:T(8,128)}, s32[]{:T(128)}, s32[]{:T(128)}, s32[]{:T(128)}, /*index=5*/f32[2,255,128]{2,1,0:T(8,128)S(1)}, f32[2,12...) while((s32[]{:T(128)}, f32[512,128]{1,0:T(8,128)}, ...), condition=%wide.region_9.8_spmd, body=%wide.region_8.7_spmd.sunk | while | flops 125501192 | bytes 1243419 | solution.py:77
  931.2 1.3 fusion.30
  933.9 1.7 dynamic_update_slice.10
  936.2 1.3 fusion.30
  939.0 1.6 dynamic_update_slice.10
  941.5 1.9 collective-permute-start.1
  943.5 1.9 collective-permute-done.1
  946.3 1.9 collective-permute-start
  948.3 5.0 collective-permute-done
  954.9 11.8 %collective-permute-start.1 = (f32[256,128]{1,0:T(8,128)S(1)}, f32[256,128]{1,0:T(8,128)S(1)}, u32[]{:S(2)}, u32[]{:S(2)}) collective-permute-start(f32[256,128]{1,0:T(8,128)S(1)} %slice.110), channel_id=1, source_target_pairs={{0,32},{32,64},{64,96},{96,128},{128,160},{160,192},{192,224},{224... | collective-permute-start | bytes 393224 | tf_op jit(solution)/shard_map/while/body/eval_jaxpr/ppermute | solution.py:17
  966.8 1.9 collective-permute-done.1
  969.6 1.9 collective-permute-start
  971.6 5.0 collective-permute-done
  978.3 1.9 collective-permute-start.1
  980.2 1.9 collective-permute-done.1
  (113 shorter events, 74.6 us)
Async XLA Ops:
  6.5 0.9 copy-start.4
  6.5 0.7 copy-start.6
  7.5 0.8 copy-start.3
  7.5 0.8 copy-start.5
  8.3 603.7 %copy-start.1 = (f32[256,128]{1,0:T(8,128)S(1)}, f32[256,128]{1,0:T(8,128)}, u32[]{:S(2)}) copy-start(f32[256,128]{1,0:T(8,128)} %param.21) | copy-start | bytes 393220
  8.3 294.5 %all-reduce.6.cloned.1.call-start = ((), (), s32[]{:S(2)}) async-start(), calls=%async_computation | async-start | bytes 393216 | tf_op jit(solution)/shard_map/while/body/eval_jaxpr/psum | solution.py:11
  302.8 1.5 copy-start.2
  305.0 305.0 %all-reduce.6.cloned.1.call-start = ((), (), s32[]{:S(2)}) async-start(), calls=%async_computation | async-start | bytes 393216 | tf_op jit(solution)/shard_map/while/body/eval_jaxpr/psum | solution.py:11
  609.9 1.5 copy-start.2
  612.1 25.9 %collective-permute-start = (f32[256,128]{1,0:T(8,128)S(1)}, f32[256,128]{1,0:T(8,128)S(1)}, u32[]{:S(2)}, u32[]{:S(2)}) collective-permute-start(f32[256,128]{1,0:T(8,128)S(1)} %get-tuple-element.970), channel_id=1, source_target_pairs={{32,0},{64,32},{96,64},{128,96},{160,128},{192,160},{224,192},{256... | collective-permute-start | bytes 393224 | tf_op jit(solution)/shard_map/while/body/eval_jaxpr/ppermute | solution.py:17
  639.6 3.9 collective-permute-start.1
  644.4 7.0 collective-permute-start
  653.0 3.9 collective-permute-start.1
  657.8 7.0 collective-permute-start
  666.5 4.2 collective-permute-start.1
  671.6 7.5 collective-permute-start
  680.7 4.3 collective-permute-start.1
  686.0 7.5 collective-permute-start
  695.0 4.3 collective-permute-start.1
  700.3 7.5 collective-permute-start
  709.4 4.3 collective-permute-start.1
  714.6 7.5 collective-permute-start
  723.7 4.3 collective-permute-start.1
  728.9 7.5 collective-permute-start
  738.0 11.2 %collective-permute-start.1 = (f32[256,128]{1,0:T(8,128)S(1)}, f32[256,128]{1,0:T(8,128)S(1)}, u32[]{:S(2)}, u32[]{:S(2)}) collective-permute-start(f32[256,128]{1,0:T(8,128)S(1)} %slice.110), channel_id=1, source_target_pairs={{0,32},{32,64},{64,96},{96,128},{128,160},{160,192},{192,224},{224... | collective-permute-start | bytes 393224 | tf_op jit(solution)/shard_map/while/body/eval_jaxpr/ppermute | solution.py:17
  750.2 18.6 %collective-permute-start = (f32[256,128]{1,0:T(8,128)S(1)}, f32[256,128]{1,0:T(8,128)S(1)}, u32[]{:S(2)}, u32[]{:S(2)}) collective-permute-start(f32[256,128]{1,0:T(8,128)S(1)} %get-tuple-element.970), channel_id=1, source_target_pairs={{32,0},{64,32},{96,64},{128,96},{160,128},{192,160},{224,192},{256... | collective-permute-start | bytes 393224 | tf_op jit(solution)/shard_map/while/body/eval_jaxpr/ppermute | solution.py:17
  770.4 13.2 %collective-permute-start.1 = (f32[256,128]{1,0:T(8,128)S(1)}, f32[256,128]{1,0:T(8,128)S(1)}, u32[]{:S(2)}, u32[]{:S(2)}) collective-permute-start(f32[256,128]{1,0:T(8,128)S(1)} %slice.110), channel_id=1, source_target_pairs={{0,32},{32,64},{64,96},{96,128},{128,160},{160,192},{192,224},{224... | collective-permute-start | bytes 393224 | tf_op jit(solution)/shard_map/while/body/eval_jaxpr/ppermute | solution.py:17
  784.6 18.5 %collective-permute-start = (f32[256,128]{1,0:T(8,128)S(1)}, f32[256,128]{1,0:T(8,128)S(1)}, u32[]{:S(2)}, u32[]{:S(2)}) collective-permute-start(f32[256,128]{1,0:T(8,128)S(1)} %get-tuple-element.970), channel_id=1, source_target_pairs={{32,0},{64,32},{96,64},{128,96},{160,128},{192,160},{224,192},{256... | collective-permute-start | bytes 393224 | tf_op jit(solution)/shard_map/while/body/eval_jaxpr/ppermute | solution.py:17
  804.7 13.5 %collective-permute-start.1 = (f32[256,128]{1,0:T(8,128)S(1)}, f32[256,128]{1,0:T(8,128)S(1)}, u32[]{:S(2)}, u32[]{:S(2)}) collective-permute-start(f32[256,128]{1,0:T(8,128)S(1)} %slice.110), channel_id=1, source_target_pairs={{0,32},{32,64},{64,96},{96,128},{128,160},{160,192},{192,224},{224... | collective-permute-start | bytes 393224 | tf_op jit(solution)/shard_map/while/body/eval_jaxpr/ppermute | solution.py:17
  819.1 18.0 %collective-permute-start = (f32[256,128]{1,0:T(8,128)S(1)}, f32[256,128]{1,0:T(8,128)S(1)}, u32[]{:S(2)}, u32[]{:S(2)}) collective-permute-start(f32[256,128]{1,0:T(8,128)S(1)} %get-tuple-element.970), channel_id=1, source_target_pairs={{32,0},{64,32},{96,64},{128,96},{160,128},{192,160},{224,192},{256... | collective-permute-start | bytes 393224 | tf_op jit(solution)/shard_map/while/body/eval_jaxpr/ppermute | solution.py:17
  838.8 13.8 %collective-permute-start.1 = (f32[256,128]{1,0:T(8,128)S(1)}, f32[256,128]{1,0:T(8,128)S(1)}, u32[]{:S(2)}, u32[]{:S(2)}) collective-permute-start(f32[256,128]{1,0:T(8,128)S(1)} %slice.110), channel_id=1, source_target_pairs={{0,32},{32,64},{64,96},{96,128},{128,160},{160,192},{192,224},{224... | collective-permute-start | bytes 393224 | tf_op jit(solution)/shard_map/while/body/eval_jaxpr/ppermute | solution.py:17
  853.5 17.9 %collective-permute-start = (f32[256,128]{1,0:T(8,128)S(1)}, f32[256,128]{1,0:T(8,128)S(1)}, u32[]{:S(2)}, u32[]{:S(2)}) collective-permute-start(f32[256,128]{1,0:T(8,128)S(1)} %get-tuple-element.970), channel_id=1, source_target_pairs={{32,0},{64,32},{96,64},{128,96},{160,128},{192,160},{224,192},{256... | collective-permute-start | bytes 393224 | tf_op jit(solution)/shard_map/while/body/eval_jaxpr/ppermute | solution.py:17
  873.1 14.1 %collective-permute-start.1 = (f32[256,128]{1,0:T(8,128)S(1)}, f32[256,128]{1,0:T(8,128)S(1)}, u32[]{:S(2)}, u32[]{:S(2)}) collective-permute-start(f32[256,128]{1,0:T(8,128)S(1)} %slice.110), channel_id=1, source_target_pairs={{0,32},{32,64},{64,96},{96,128},{128,160},{160,192},{192,224},{224... | collective-permute-start | bytes 393224 | tf_op jit(solution)/shard_map/while/body/eval_jaxpr/ppermute | solution.py:17
  888.1 17.5 %collective-permute-start = (f32[256,128]{1,0:T(8,128)S(1)}, f32[256,128]{1,0:T(8,128)S(1)}, u32[]{:S(2)}, u32[]{:S(2)}) collective-permute-start(f32[256,128]{1,0:T(8,128)S(1)} %get-tuple-element.970), channel_id=1, source_target_pairs={{32,0},{64,32},{96,64},{128,96},{160,128},{192,160},{224,192},{256... | collective-permute-start | bytes 393224 | tf_op jit(solution)/shard_map/while/body/eval_jaxpr/ppermute | solution.py:17
  907.2 14.3 %collective-permute-start.1 = (f32[256,128]{1,0:T(8,128)S(1)}, f32[256,128]{1,0:T(8,128)S(1)}, u32[]{:S(2)}, u32[]{:S(2)}) collective-permute-start(f32[256,128]{1,0:T(8,128)S(1)} %slice.110), channel_id=1, source_target_pairs={{0,32},{32,64},{64,96},{96,128},{128,160},{160,192},{192,224},{224... | collective-permute-start | bytes 393224 | tf_op jit(solution)/shard_map/while/body/eval_jaxpr/ppermute | solution.py:17
  922.5 7.3 collective-permute-start
  941.5 3.9 collective-permute-start.1
  946.3 7.0 collective-permute-start
  954.9 13.8 %collective-permute-start.1 = (f32[256,128]{1,0:T(8,128)S(1)}, f32[256,128]{1,0:T(8,128)S(1)}, u32[]{:S(2)}, u32[]{:S(2)}) collective-permute-start(f32[256,128]{1,0:T(8,128)S(1)} %slice.110), channel_id=1, source_target_pairs={{0,32},{32,64},{64,96},{96,128},{128,160},{160,192},{192,224},{224... | collective-permute-start | bytes 393224 | tf_op jit(solution)/shard_map/while/body/eval_jaxpr/ppermute | solution.py:17
  969.6 7.0 collective-permute-start
  978.3 3.9 collective-permute-start.1
  983.1 0.7 copy-start
Sparse Core Ops, SparseCore 0:
  12.1 290.6 all-reduce.5
  308.8 301.1 all-reduce.5
where the time goes:
time: 999 us; the launch traced here: 991 us
  waiting for transfers between devices  708 us (71%)
  starting transfers between devices  203 us (20%)
  other arithmetic  34.5 us (3%)
  local copies, waits for them, and re-layouts  21.5 us (2%)
  between operations  13.5 us (1%)
    psum x2, waiting for transfers between devices, from_root(): return lax.psum(jnp.where(mine, value, jnp.zeros_like(value)), axis)  593 us
    ppermute x32, starting transfers between devices, from_behind(): return lax.ppermute(value, axis, pairs)  203 us
    ppermute x32, waiting for transfers between devices, from_behind(): return lax.ppermute(value, axis, pairs)  116 us
  transfers between devices with their start and end apart: 34, of which 34 were waited for; matrix products, arithmetic and copies ran while one was open for 0% of the time, Pallas kernels for 0%

commit v1 on v0

v1 whole, which is shorter than its diff:
```python
import functools

import jax
import jax.numpy as jnp
from jax import lax
from jax.experimental import pallas as pl
from jax.experimental.pallas import tpu as pltpu
from jax.sharding import PartitionSpec as P

MESH = pl.DeviceIdType.MESH
F32 = jnp.float32
BF16 = jnp.bfloat16


def split(a):
    hi = a.astype(BF16)
    return hi, (a - hi.astype(F32)).astype(BF16)


def mm(a, b, rhs_t=False):
    dims = (((1,), (1 if rhs_t else 0,)), ((), ()))
    ah, al = split(a)
    bh, bl = split(b)
    dot = functools.partial(
        lax.dot_general, dimension_numbers=dims, preferred_element_type=F32
    )
    return dot(ah, bl) + dot(al, bh) + dot(ah, bh)


def both(pair):
    return jnp.concatenate([pair[0], pair[1]], axis=1)


def far_first(cols):
    inner = 4 if cols % 4 == 0 else 1
    outer = cols // inner
    found = []
    for dz in range(outer):
        for dy in range(inner):
            if dz or dy:
                found.append((min(dz, outer - dz) + 2 * min(dy, inner - dy), dz, dy))
    found.sort(reverse=True)
    return inner, outer, [(dz, dy) for _, dz, dy in found]


def kernel(
    rows, cols, off_ref, plan_ref, e_ref, v_ref, t_ref, y_ref,
    xin, vbuf, tbuf, mine, g1, stage, g2, ebuf, p1buf, fbuf, abuf, hbuf, bbuf, sbuf, smbuf, srecv, cbuf, dbuf,
    lsem, hsem, s1, s2, psem, asem, bsend, brecv, dsem,
):
    nb = t_ref.shape[1]
    part = nb // rows
    own = e_ref.shape[0]
    r = lax.axis_index("row")
    c = lax.axis_index("col")
    core, pair, x = r % 2, (r // 2) % 2, r // 4
    groups = rows // 4
    inner, outer, spread = far_first(cols)
    blocks = 2 * rows - 2

    def col_at(dz, dy):
        return lax.rem(c // inner + dz, outer) * inner + lax.rem(c % inner + dy, inner)

    def row_at(k):
        return lax.rem(r + k, rows)

    def remote(src, dst, send, recv, to_row, to_col):
        return pltpu.make_async_remote_copy(
            src_ref=src, dst_ref=dst, send_sem=send, recv_sem=recv,
            device_id=(to_row, to_col), device_id_type=MESH,
        )

    barrier = pltpu.get_barrier_semaphore()
    for dz, dy in spread:
        pl.semaphore_signal(barrier, 1, device_id=(r, col_at(dz, dy)), device_id_type=MESH)
    for k in range(1, rows):
        pl.semaphore_signal(barrier, 1, device_id=(row_at(k), c), device_id_type=MESH)

    vbuf[2 * nb - 1 : 2 * nb] = jnp.zeros((1, nb), F32)
    xin[0:nb] = jnp.zeros((nb, nb), F32)
    get_v = pltpu.make_async_copy(v_ref.at[0], vbuf.at[pl.ds(0, 2 * nb - 1)], lsem.at[0])
    get_t = pltpu.make_async_copy(t_ref.at[0], tbuf, lsem.at[1])
    get_e = pltpu.make_async_copy(e_ref, xin.at[pl.ds(nb, own)], lsem.at[2])
    get_v.start()
    get_t.start()
    get_e.start()
    get_v.wait()
    get_t.wait()
    at = pl.multiple_of(r * part, part)
    row_ids = lax.broadcasted_iota(jnp.int32, (part, nb), 0) + at
    col_ids = lax.broadcasted_iota(jnp.int32, (part, nb), 1)
    mine[0:part] = jnp.where(
        row_ids >= col_ids, vbuf[pl.ds(at, part)], vbuf[pl.ds(nb + at, part)]
    )
    mine[part : 2 * part] = tbuf[pl.ds(at, part)]
    g1[c] = mine[...]

    pl.semaphore_wait(barrier, cols - 1 + rows - 1)

    for dz, dy in spread:
        remote(mine, g1.at[c], s1.at[0], s1.at[1], r, col_at(dz, dy)).start()
    head = remote(
        e_ref, xin.at[pl.ds(nb + own, own)], hsem.at[0], hsem.at[1], row_at(rows - 1), c
    )
    head.start()
    got1 = g1.at[pl.ds(0, cols - 1)]
    pltpu.make_async_copy(got1, got1, s1.at[1]).wait()

    order = sorted(range(1, rows), key=lambda k: -min(k, rows - k)) + [0]
    for k in order:
        to = row_at(k)
        for j in range(3):
            block = jnp.clip(2 * to - 1 + j, 0, blocks - 1)
            picked = g1[plan_ref[0, block]]
            if k:
                stage[k, 2 * part * j : 2 * part * (j + 1)] = picked
            else:
                g2[r, 2 * part * j : 2 * part * (j + 1)] = picked
        if k:
            remote(stage.at[k], g2.at[r], s2.at[0], s2.at[1], to, c).start()

    get_e.wait()
    head.wait_recv()
    off = off_ref[0]
    s0 = xin[pl.ds(off, nb)]
    fresh = [xin[pl.ds(off + nb * (1 + j), nb)] for j in range(3)]

    got2 = g2.at[pl.ds(0, rows - 1)]
    pltpu.make_async_copy(got2, got2, s2.at[1]).wait()

    ri = lax.broadcasted_iota(jnp.int32, (nb, nb), 0)
    ci = lax.broadcasted_iota(jnp.int32, (nb, nb), 1)
    eye = (ri == ci).astype(F32)
    maps = []
    for j in range(3):
        number = 2 * r - 1 + j
        live = ((number >= 0) & (number < blocks)).astype(F32)
        lo = 2 * part * j
        packed = g2[:, lo : lo + part].reshape(nb, nb)
        factor = g2[:, lo + part : lo + 2 * part].reshape(nb, nb) * live
        lower = jnp.where(ri >= ci, packed, 0.0)
        upper = jnp.where(ri >= ci, 0.0, packed)
        vectors = jnp.concatenate([lower, upper], axis=0)
        tv = mm(factor, vectors, rhs_t=True)
        m, n = tv[:, :nb], tv[:, nb:]
        z = mm(n, fresh[j])
        w = mm(vectors, jnp.concatenate([m, z], axis=1))
        maps.append((eye - w[:nb, :nb], -w[:nb, nb:], -w[nb:, :nb], fresh[j] - w[nb:, nb:]))
    (c0, d0, a0, b0), (c1, d1, a1, b1), (c2, d2, a2, b2) = maps
    w = mm(jnp.concatenate([c1, a1], axis=0), jnp.concatenate([a0, b0], axis=1))
    cbuf[0:nb] = c0
    dbuf[0:nb] = d0
    cbuf[nb : 2 * nb] = w[:nb, :nb]
    dbuf[nb : 2 * nb] = w[:nb, nb:] + d1
    ebuf[0] = w[nb:, :nb]
    ebuf[1] = w[nb:, nb:] + b1

    to_core1 = remote(ebuf, p1buf, psem.at[0], psem.at[1], r ^ 1, c)
    to_pair = remote(fbuf, abuf, asem.at[0], asem.at[1], r ^ 2, c)
    to_core0 = remote(smbuf, srecv, dsem.at[0], dsem.at[1], r ^ 1, c)

    @pl.when(core == 0)
    def _():
        to_core1.start()

    w = mm(c2, both(ebuf))
    cbuf[2 * nb : 3 * nb] = w[:, :nb]
    dbuf[2 * nb : 3 * nb] = w[:, nb:] + d2

    def along_x(step, half):
        return remote(
            hbuf.at[half], bbuf.at[x, half], bsend.at[step, half], brecv.at[x, half],
            lax.rem(r + 4 * step, rows), c,
        )

    def from_x(source, half):
        slot = bbuf.at[source, half]
        return pltpu.make_async_copy(slot, slot, brecv.at[source, half])

    @pl.when(core == 1)
    def _():
        to_core1.wait_recv()
        w = mm(ebuf[0], both(p1buf))
        fbuf[0] = w[:, :nb]
        fbuf[1] = w[:, nb:] + ebuf[1]
        to_pair.start()
        to_pair.wait_recv()
        first = pair == 0
        late_g = jnp.where(first, abuf[0], fbuf[0])
        late_b = jnp.where(first, abuf[1], fbuf[1])
        early = jnp.where(first, both(fbuf), both(abuf))
        w = mm(late_g, early)
        hbuf[0] = w[:, :nb]
        hbuf[1] = w[:, nb:] + late_b
        for step in range(1, groups):
            @pl.when(x + step < groups)
            def _(step=step):
                along_x(step, 1).start()

                @pl.when(x > 0)
                def _():
                    along_x(step, 0).start()

        @pl.when(x == 0)
        def _():
            sbuf[...] = s0

        for source in range(groups - 1):
            @pl.when(x > source)
            def _(source=source):
                from_x(source, 1).wait()
                if source:
                    from_x(source, 0).wait()
                    sbuf[...] = mm(bbuf[source, 0], sbuf[...]) + bbuf[source, 1]
                else:
                    sbuf[...] = bbuf[source, 1]

        @pl.when(pair == 0)
        def _():
            smbuf[...] = sbuf[...]

        @pl.when(pair == 1)
        def _():
            smbuf[...] = mm(abuf[0], sbuf[...]) + abuf[1]

        to_core0.start()
        sbuf[...] = mm(p1buf[0], smbuf[...]) + p1buf[1]

    @pl.when(core == 0)
    def _():
        to_core0.wait_recv()
        sbuf[...] = jnp.where(r == 0, s0, srecv[...])

    y_ref[...] = mm(cbuf[...], sbuf[...]) + dbuf[...]

    pltpu.make_async_copy(got1, got1, s1.at[0]).wait()
    pltpu.make_async_copy(got2, got2, s2.at[0]).wait()
    head.wait_send()

    @pl.when(core == 0)
    def _():
        to_core1.wait_send()

    @pl.when(core == 1)
    def _():
        to_pair.wait_send()
        to_core0.wait_send()
        for step in range(1, groups):
            @pl.when(x + step < groups)
            def _(step=step):
                along_x(step, 1).wait_send()

                @pl.when(x > 0)
                def _():
                    along_x(step, 0).wait_send()


def solution(mesh):
    rows, cols = mesh.shape["row"], mesh.shape["col"]

    def on_device(eigvecs, offsets, plan, refl_v, refl_t):
        own, width = eigvecs.shape
        nb = refl_t.shape[1]
        part = nb // rows
        dma = pltpu.SemaphoreType.DMA
        square = (nb, nb)
        y = pl.pallas_call(
            functools.partial(kernel, rows, cols),
            out_shape=jax.ShapeDtypeStruct((3 * nb, width), F32),
            in_specs=[
                pl.BlockSpec(memory_space=pltpu.SMEM),
                pl.BlockSpec(memory_space=pltpu.SMEM),
                pl.BlockSpec(memory_space=pl.ANY),
                pl.BlockSpec(memory_space=pl.ANY),
                pl.BlockSpec(memory_space=pl.ANY),
            ],
            out_specs=pl.BlockSpec(memory_space=pltpu.VMEM),
            scratch_shapes=[
                pltpu.VMEM((nb + 2 * own, width), F32),
                pltpu.VMEM((2 * nb, nb), F32),
                pltpu.VMEM(square, F32),
                pltpu.VMEM((2 * part, nb), F32),
                pltpu.VMEM((cols, 2 * part, nb), F32),
                pltpu.VMEM((rows, 6 * part, nb), F32),
                pltpu.VMEM((rows, 6 * part, nb), F32),
                pltpu.VMEM((2,) + square, F32),
                pltpu.VMEM((2,) + square, F32),
                pltpu.VMEM((2,) + square, F32),
                pltpu.VMEM((2,) + square, F32),
                pltpu.VMEM((2,) + square, F32),
                pltpu.VMEM((rows // 4, 2) + square, F32),
                pltpu.VMEM(square, F32),
                pltpu.VMEM(square, F32),
                pltpu.VMEM(square, F32),
                pltpu.VMEM((3 * nb, nb), F32),
                pltpu.VMEM((3 * nb, width), F32),
                dma((3,)), dma((2,)), dma((2,)), dma((2,)), dma((2,)), dma((2,)),
                dma((rows // 4, 2)), dma((rows // 4, 2)), dma((2,)),
            ],
            compiler_params=pltpu.CompilerParams(
                collective_id=0, has_side_effects=True, vmem_limit_bytes=24 * 2**20
            ),
            cost_estimate=pl.CostEstimate(
                flops=2 * 30 * nb**3, bytes_accessed=4 * 10 * nb * nb, transcendentals=0
            ),
            name="chase",
        )(offsets, plan, eigvecs, refl_v, refl_t)
        return lax.dynamic_slice(y, (nb - offsets[0], 0), (own, width))

    return jax.shard_map(
        on_device,
        mesh=mesh,
        in_specs=(P("row", "col"), P(), P(), P("col", None, None), P("col", None, None)),
        out_specs=P("row", "col"),
        check_vma=False,
    )
```

time: 999 us -> 44.7 us (0.04)
  waiting for transfers between devices: 708 us -> 0 us
  starting transfers between devices: 203 us -> 0 us
  Pallas kernels: 0 us -> 42.2 us
  other arithmetic: 34.5 us -> 0 us
  local copies, waits for them, and re-layouts: 21.5 us -> 1.64 us
  between operations: 13.5 us -> 0.72 us
    psum x2 -> x0, waiting for transfers between devices: 593 us -> none  [from_root(): return lax.psum(jnp.where(mine, value, jnp.zeros_like(value)), axis)]
    ppermute x32 -> x0, starting transfers between devices: 203 us -> none  [from_behind(): return lax.ppermute(value, axis, pairs)]
    ppermute x32 -> x0, waiting for transfers between devices: 116 us -> none  [from_behind(): return lax.ppermute(value, axis, pairs)]
    pallas_call x0 -> x1, Pallas kernels: none -> 42.2 us  [on_device(): pl.pallas_call(functools.partial(kernel, rows, cols), out_shape=jax.Shape...]
    select_n x20 -> x0, other arithmetic: 17.3 us -> none  [the longest x16 14.7 us: run_tick(): new_head = jnp.where(sender_live, returned, matrix)]
    slice x16 -> x0, local copies, waits for them, and re-layouts: 14.6 us -> none  [run_tick(): returned = from_behind(extended[rows_dev:], 'row', 1)]
    concatenate x16 -> x0, other arithmetic: 11.5 us -> none  [the longest x15 10.8 us: unchanged(): return jnp.concatenate([current, fetched], 0)]
  transfers between devices with their start and end apart: 34 -> 0, of which waited for: 34 -> 0; matrix products, arithmetic and copies ran while one was open for 0% -> 0% of each run, Pallas kernels for 0% -> 0%
where the time goes in v1:
time: 44.7 us; the launch traced here: 44.6 us
  Pallas kernels  42.2 us (94%)
  local copies, waits for them, and re-layouts  1.64 us (4%)
  between operations  0.72 us (2%)
    pallas_call x1, Pallas kernels, on_device(): pl.pallas_call(functools.partial(kernel, rows, cols), out_shape=jax.Shape...  42.2 us
    unnamed x7, local copies, waits for them, and re-layouts  0.97 us

profile of v1, /device:TPU:7, one launch (start us, length us, event | category | flops | bytes accessed | tf_op | source)
XLA Modules:
  0.0 44.6 jit_solution(12410190946172450021)
XLA Ops:
  0.7 0.0 copy-start
  0.7 0.0 copy-start.1
  0.7 0.0 copy-start.2
  0.7 1.0 %copy.6.v_ref = f32[1,255,128]{2,1,0:T(8,128)S(1)} copy(f32[1,255,128]{2,0,1:T(1,128)} %param.8) | data formatting | bytes 261120 | tf_op args[3]
  1.6 0.0 copy-done
  1.7 0.0 copy-done.1
  1.7 0.0 copy-done.2
  1.7 42.2 %chase.1 = f32[384,128]{1,0:T(8,128)S(1)} custom-call(s32[1]{0:T(128)S(6)} %copy.7.off_ref, s32[1,30]{1,0:T(1,128)S(1)} %copy-done.2, f32[256,128]{1,0:T(8,128)S(1)} %copy-done, f32[1,255,128]{2,1,0:T(8,128)S(1)} %copy.6.v_ref, f32[1,128,128]{2,1,0:T(8,128)S(1)} %copy-done.1), custom_call_target="tpu_custom_call" | custom-call | flops 125829120 | bytes 655360 | tf_op jit(solution)/shard_map/chase/pallas_call | solution.py:267
  43.9 0.7 %constant_dynamic-slice_fusion = f32[256,128]{1,0:T(8,128)} fusion(f32[384,128]{1,0:T(8,128)S(1)} %chase.1, s32[]{:T(128)S(6)} %select_n.3), kind=kLoop, calls=%fused_computation | loop fusion | bytes 262148 | tf_op jit(solution)/shard_map/dynamic_slice | solution.py:308
Async XLA Ops:
  0.7 1.0 %copy-start = (f32[256,128]{1,0:T(8,128)S(1)}, f32[256,128]{1,0:T(8,128)}, u32[]{:S(2)}) copy-start(f32[256,128]{1,0:T(8,128)} %e_ref.1) | copy-start | bytes 393220
  0.7 1.0 %copy-start.1 = (f32[1,128,128]{2,1,0:T(8,128)S(1)}, f32[1,128,128]{2,1,0:T(8,128)}, u32[]{:S(2)}) copy-start(f32[1,128,128]{2,1,0:T(8,128)} %t_ref.1) | copy-start | bytes 196612
  0.7 1.0 %copy-start.2 = (s32[1,30]{1,0:T(1,128)S(1)}, s32[1,30]{1,0:T(1,128)}, u32[]{:S(2)}) copy-start(s32[1,30]{1,0:T(1,128)} %plan_ref.1) | copy-start | bytes 364

commit v2 on v1

v2 whole, which is shorter than its diff:
```python
import functools

import jax
import jax.numpy as jnp
from jax import lax
from jax.experimental import pallas as pl
from jax.experimental.pallas import tpu as pltpu
from jax.sharding import PartitionSpec as P

MESH = pl.DeviceIdType.MESH
F32 = jnp.float32
BF16 = jnp.bfloat16


def split(a):
    hi = a.astype(BF16)
    return hi, (a - hi.astype(F32)).astype(BF16)


def mm(a, b, rhs_t=False):
    dims = (((1,), (1 if rhs_t else 0,)), ((), ()))
    ah, al = split(a)
    bh, bl = split(b)
    dot = functools.partial(
        lax.dot_general, dimension_numbers=dims, preferred_element_type=F32
    )
    return dot(ah, bl) + dot(al, bh) + dot(ah, bh)


def both(pair):
    return jnp.concatenate([pair[0], pair[1]], axis=1)


def classes(cols):
    if cols == 32:
        start_z = (0.0, 0.9, 1.9, 2.8, 5.8, 6.7, 7.6, 8.4)
        start_y = (0.4, 2.2, 4.7, 3.3)
        start = {4 * z + y: start_z[z] + start_y[y] for z in range(8) for y in range(4)}
        served = {(7, 0): (6, 0), (5, 1): (4, 1), (6, 1): (5, 0), (7, 1): (0, 1)}
        for y in (2, 3):
            served.update({(4 + k, y): (3 - k, y) for k in range(4)})
        partner = {4 * a + b: 4 * d + e for (a, b), (d, e) in served.items()}
    else:
        start = {k: k for k in range(cols)}
        partner = {k: k - cols // 2 for k in range((cols + 1) // 2, cols)}
    order = sorted(start, key=lambda k: start[k])
    return [k for k in order if k not in partner], partner


def kernel(
    rows, cols, off_ref, plan_ref, e_ref, v_ref, t_ref, y_ref,
    xin, vbuf, tbuf, mine, g1, stage, stage3, g2, g3, ebuf, p1buf, fbuf, abuf, hbuf, bbuf, pbuf, sbuf, cbuf, dbuf,
    lsem, hsem, s1, s2, s3, psem, asem, bsend, brecv, dsem, qsem, rowsem,
):
    nb = t_ref.shape[1]
    part = nb // rows
    own = e_ref.shape[0]
    r = lax.axis_index("row")
    c = lax.axis_index("col")
    core, pair, x = r % 2, (r // 2) % 2, r // 4
    groups = rows // 4
    early, partner = classes(cols)
    blocks = 2 * rows - 2

    is_late = functools.reduce(jnp.logical_or, [c == k for k in partner])
    serves = functools.reduce(jnp.logical_or, [c == k for k in partner.values()])
    other = sum(
        jnp.where(c == a, b, 0) + jnp.where(c == b, a, 0) for a, b in partner.items()
    )
    is_early = jnp.logical_not(is_late)

    def row_at(k):
        return lax.rem(r + k, rows)

    def remote(src, dst, send, recv, to_row, to_col):
        return pltpu.make_async_remote_copy(
            src_ref=src, dst_ref=dst, send_sem=send, recv_sem=recv,
            device_id=(to_row, to_col), device_id_type=MESH,
        )

    def signal(sem, to_row, to_col):
        pl.semaphore_signal(sem, 1, device_id=(to_row, to_col), device_id_type=MESH)

    def await_bytes(ref, sem):
        pltpu.make_async_copy(ref, ref, sem).wait()

    vbuf[2 * nb - 1 : 2 * nb] = jnp.zeros((1, nb), F32)
    get_v = pltpu.make_async_copy(v_ref.at[0], vbuf.at[pl.ds(0, 2 * nb - 1)], lsem.at[0])
    get_t = pltpu.make_async_copy(t_ref.at[0], tbuf, lsem.at[1])
    get_e = pltpu.make_async_copy(e_ref, xin.at[pl.ds(nb, own)], lsem.at[2])
    get_v.start()
    get_t.start()
    get_e.start()

    barrier = pltpu.get_barrier_semaphore()

    @pl.when(is_early)
    def _():
        for k in list(partner) + early[::-1]:
            @pl.when(c != k)
            def _(k=k):
                signal(barrier, r, k)
        for k in range(1, rows):
            signal(barrier, row_at(k), c)

        @pl.when(serves)
        def _():
            for k in range(1, rows):
                signal(barrier, row_at(k), other)

    xin[0:nb] = jnp.zeros((nb, nb), F32)
    get_v.wait()
    get_t.wait()
    at = pl.multiple_of(r * part, part)
    row_ids = lax.broadcasted_iota(jnp.int32, (part, nb), 0) + at
    col_ids = lax.broadcasted_iota(jnp.int32, (part, nb), 1)
    mine[0:part] = jnp.where(
        row_ids >= col_ids, vbuf[pl.ds(at, part)], vbuf[pl.ds(nb + at, part)]
    )
    mine[part : 2 * part] = tbuf[pl.ds(at, part)]

    pl.semaphore_wait(barrier, len(early) + rows - 1 - is_early.astype(jnp.int32))

    for k in early:
        @pl.when(c != k)
        def _(k=k):
            remote(mine, g1.at[c], s1.at[0], s1.at[1], r, k).start()

    head = remote(
        e_ref, xin.at[pl.ds(nb + own, own)], hsem.at[0], hsem.at[1], row_at(rows - 1), c
    )

    @pl.when(is_early)
    def _():
        head.start()
        g1[c] = mine[...]
        await_bytes(g1.at[pl.ds(0, cols - 1)], s1.at[1])

    @pl.when(is_late)
    def _():
        for k in range(1, rows):
            signal(rowsem, row_at(k), other)
        await_bytes(g1, s1.at[1])
        head.start()

    order = sorted(range(1, rows), key=lambda k: -min(k, rows - k)) + [0]

    def pick(to, j):
        return g1[plan_ref[0, jnp.clip(2 * to - 1 + j, 0, blocks - 1)]]

    for k in order:
        to = row_at(k)
        dst = stage.at[k] if k else g2.at[r]
        dst[0 : 2 * part] = pick(to, 0)
        dst[2 * part : 4 * part] = pick(to, 1)
        if k:
            remote(stage.at[k], g2.at[r], s2.at[0], s2.at[1], to, c).start()

    relay = remote(g1, g1, qsem.at[0], s1.at[1], r, other)

    @pl.when(serves)
    def _():
        pl.semaphore_wait(rowsem, rows - 1)
        relay.start()

    for k in order:
        to = row_at(k)
        dst = stage3.at[k] if k else g3.at[r]
        dst[...] = pick(to, 2)
        if k:
            remote(stage3.at[k], g3.at[r], s3.at[0], s3.at[1], to, c).start()

    get_e.wait()
    head.wait_recv()
    off = off_ref[0]
    s0 = xin[pl.ds(off, nb)]

    ri = lax.broadcasted_iota(jnp.int32, (nb, nb), 0)
    ci = lax.broadcasted_iota(jnp.int32, (nb, nb), 1)
    eye = (ri == ci).astype(F32)

    def block_map(j, packed, factor):
        number = 2 * r - 1 + j
        live = ((number >= 0) & (number < blocks)).astype(F32)
        fresh = xin[pl.ds(off + nb * (1 + j), nb)]
        packed = packed.reshape(nb, nb)
        factor = factor.reshape(nb, nb) * live
        lower = jnp.where(ri >= ci, packed, 0.0)
        upper = jnp.where(ri >= ci, 0.0, packed)
        vectors = jnp.concatenate([lower, upper], axis=0)
        tv = mm(factor, vectors, rhs_t=True)
        m, n = tv[:, :nb], tv[:, nb:]
        z = mm(n, fresh)
        w = mm(vectors if j < 2 else lower, jnp.concatenate([m, z], axis=1))
        if j == 2:
            return eye - w[:, :nb], -w[:, nb:]
        return eye - w[:nb, :nb], -w[:nb, nb:], -w[nb:, :nb], fresh - w[nb:, nb:]

    await_bytes(g2.at[pl.ds(0, rows - 1)], s2.at[1])
    c0, d0, a0, b0 = block_map(0, g2[:, 0:part], g2[:, part : 2 * part])
    c1, d1, a1, b1 = block_map(1, g2[:, 2 * part : 3 * part], g2[:, 3 * part : 4 * part])
    w = mm(jnp.concatenate([a1, c1], axis=0), jnp.concatenate([a0, b0], axis=1))
    ebuf[0] = w[:nb, :nb]
    ebuf[1] = w[:nb, nb:] + b1

    to_core1 = remote(ebuf, p1buf, psem.at[0], psem.at[1], r ^ 1, c)
    to_pair = remote(fbuf, abuf, asem.at[0], asem.at[1], r ^ 2, c)
    prefix = remote(abuf, pbuf, psem.at[0], psem.at[1], r ^ 1, c)
    state = remote(sbuf, sbuf, dsem.at[0], dsem.at[1], r ^ 1, c)
    core0, core1 = core == 0, core == 1

    @pl.when(core0)
    def _():
        to_core1.start()

    cbuf[0:nb] = c0
    dbuf[0:nb] = d0
    cbuf[nb : 2 * nb] = w[nb:, :nb]
    dbuf[nb : 2 * nb] = w[nb:, nb:] + d1

    @pl.when(core1)
    def _():
        to_core1.wait_recv()
        w = mm(ebuf[0], both(p1buf))
        fbuf[0] = w[:, :nb]
        fbuf[1] = w[:, nb:] + ebuf[1]
        to_pair.start()

    await_bytes(g3.at[pl.ds(0, rows - 1)], s3.at[1])
    c2, d2 = block_map(2, g3[:, 0:part], g3[:, part : 2 * part])
    w = mm(c2, both(ebuf))
    cbuf[2 * nb : 3 * nb] = w[:, :nb]
    dbuf[2 * nb : 3 * nb] = w[:, nb:] + d2

    def along_x(step, half):
        return remote(
            hbuf.at[half], bbuf.at[x, half], bsend.at[step, half], brecv.at[x, half],
            lax.rem(r + 4 * step, rows), c,
        )

    @pl.when(core1)
    def _():
        to_pair.wait_recv()
        first = pair == 0

        @pl.when(pair == 1)
        def _():
            prefix.start()

        late_g = jnp.where(first, abuf[0], fbuf[0])
        late_b = jnp.where(first, abuf[1], fbuf[1])
        early_pair = jnp.where(first, both(fbuf), both(abuf))
        w = mm(late_g, early_pair)
        hbuf[0] = w[:, :nb]
        hbuf[1] = w[:, nb:] + late_b
        for step in range(1, groups):
            @pl.when(x + step < groups)
            def _(step=step):
                along_x(step, 1).start()

                @pl.when(x > 0)
                def _():
                    along_x(step, 0).start()

        @pl.when(pair == 0)
        def _():
            pbuf[...] = p1buf[...]

        @pl.when(pair == 1)
        def _():
            w = mm(p1buf[0], both(abuf))
            pbuf[0] = w[:, :nb]
            pbuf[1] = w[:, nb:] + p1buf[1]

    @pl.when(core0 & (pair == 1))
    def _():
        prefix.wait_recv()

    @pl.when(core1 | (pair == 1))
    def _():
        w = mm(cbuf[...], both(pbuf))
        cbuf[...] = w[:, :nb]
        dbuf[...] = w[:, nb:] + dbuf[...]

    @pl.when(x == 0)
    def _():
        sbuf[...] = s0

    @pl.when((x > 0) & core1)
    def _():
        for source in range(groups - 1):
            @pl.when(x > source)
            def _(source=source):
                await_bytes(bbuf.at[source, 1], brecv.at[source, 1])
                if source:
                    await_bytes(bbuf.at[source, 0], brecv.at[source, 0])
                    sbuf[...] = mm(bbuf[source, 0], sbuf[...]) + bbuf[source, 1]
                else:
                    sbuf[...] = bbuf[source, 1]
        state.start()

    @pl.when((x > 0) & core0)
    def _():
        state.wait_recv()

    y_ref[...] = mm(cbuf[...], sbuf[...]) + dbuf[...]

    sent = g1.at[pl.ds(0, len(early) - 1)]
    await_bytes(sent, s1.at[0])
    head.wait_send()
    await_bytes(g2.at[pl.ds(0, rows - 1)], s2.at[0])
    await_bytes(g3.at[pl.ds(0, rows - 1)], s3.at[0])

    @pl.when(is_late)
    def _():
        await_bytes(g1.at[0], s1.at[0])

    @pl.when(serves)
    def _():
        relay.wait_send()

    @pl.when(core0)
    def _():
        to_core1.wait_send()

    @pl.when(core1)
    def _():
        to_pair.wait_send()

        @pl.when(pair == 1)
        def _():
            prefix.wait_send()

        @pl.when(x > 0)
        def _():
            state.wait_send()

        for step in range(1, groups):
            @pl.when(x + step < groups)
            def _(step=step):
                along_x(step, 1).wait_send()

                @pl.when(x > 0)
                def _():
                    along_x(step, 0).wait_send()


def solution(mesh):
    rows, cols = mesh.shape["row"], mesh.shape["col"]

    def on_device(eigvecs, offsets, plan, refl_v, refl_t):
        own, width = eigvecs.shape
        nb = refl_t.shape[1]
        part = nb // rows
        dma = pltpu.SemaphoreType.DMA
        square = (nb, nb)
        y = pl.pallas_call(
            functools.partial(kernel, rows, cols),
            out_shape=jax.ShapeDtypeStruct((3 * nb, width), F32),
            in_specs=[
                pl.BlockSpec(memory_space=pltpu.SMEM),
                pl.BlockSpec(memory_space=pltpu.SMEM),
                pl.BlockSpec(memory_space=pltpu.HBM),
                pl.BlockSpec(memory_space=pltpu.HBM),
                pl.BlockSpec(memory_space=pltpu.HBM),
            ],
            out_specs=pl.BlockSpec(memory_space=pltpu.VMEM),
            scratch_shapes=[
                pltpu.VMEM((nb + 2 * own, width), F32),
                pltpu.VMEM((2 * nb, nb), F32),
                pltpu.VMEM(square, F32),
                pltpu.VMEM((2 * part, nb), F32),
                pltpu.VMEM((cols, 2 * part, nb), F32),
                pltpu.VMEM((rows, 4 * part, nb), F32),
                pltpu.VMEM((rows, 2 * part, nb), F32),
                pltpu.VMEM((rows, 4 * part, nb), F32),
                pltpu.VMEM((rows, 2 * part, nb), F32),
                pltpu.VMEM((2,) + square, F32),
                pltpu.VMEM((2,) + square, F32),
                pltpu.VMEM((2,) + square, F32),
                pltpu.VMEM((2,) + square, F32),
                pltpu.VMEM((2,) + square, F32),
                pltpu.VMEM((rows // 4, 2) + square, F32),
                pltpu.VMEM((2,) + square, F32),
                pltpu.VMEM(square, F32),
                pltpu.VMEM((3 * nb, nb), F32),
                pltpu.VMEM((3 * nb, width), F32),
                dma((3,)), dma((2,)), dma((2,)), dma((2,)), dma((2,)), dma((2,)), dma((2,)),
                dma((rows // 4, 2)), dma((rows // 4, 2)), dma((2,)), dma((1,)),
                pltpu.SemaphoreType.REGULAR,
            ],
            compiler_params=pltpu.CompilerParams(
                collective_id=0, has_side_effects=True, vmem_limit_bytes=24 * 2**20
            ),
            cost_estimate=pl.CostEstimate(
                flops=2 * 30 * nb**3, bytes_accessed=4 * 10 * nb * nb, transcendentals=0
            ),
            name="chase",
        )(offsets, plan, eigvecs, refl_v, refl_t)
        return lax.dynamic_slice(y, (nb - offsets[0], 0), (own, width))

    return jax.shard_map(
        on_device,
        mesh=mesh,
        in_specs=(P("row", "col"), P(), P(), P("col", None, None), P("col", None, None)),
        out_specs=P("row", "col"),
        check_vma=False,
    )
```

time: 44.7 us -> 50.3 us (1.13)
  the two profiles are of different devices: /device:TPU:7 before, /device:TPU:415 now
where the time goes in v2:
time: 50.3 us; the launch traced here: 50.1 us
  Pallas kernels  47.8 us (95%)
  local copies, waits for them, and re-layouts  1.64 us (3%)
  between operations  0.72 us (1%)
    pallas_call x1, Pallas kernels, on_device(): pl.pallas_call(functools.partial(kernel, rows, cols), out_shape=jax.Shape...  47.8 us

profile of v2, /device:TPU:415, one launch (start us, length us, event | category | flops | bytes accessed | tf_op | source)
XLA Modules:
  0.0 50.1 jit_solution(8013452870994294702)
XLA Ops:
  0.7 0.0 copy-start
  0.7 0.0 copy-start.1
  0.7 0.0 copy-start.2
  0.7 1.0 %copy.6.v_ref = f32[1,255,128]{2,1,0:T(8,128)S(1)} copy(f32[1,255,128]{2,0,1:T(1,128)} %param.8) | data formatting | bytes 261120 | tf_op args[3]
  1.6 0.0 copy-done
  1.7 0.0 copy-done.1
  1.7 0.0 copy-done.2
  1.7 47.8 %chase.1 = f32[384,128]{1,0:T(8,128)S(1)} custom-call(s32[1]{0:T(128)S(6)} %copy.7.off_ref, s32[1,30]{1,0:T(1,128)S(1)} %copy-done.2, f32[256,128]{1,0:T(8,128)S(1)} %copy-done, f32[1,255,128]{2,1,0:T(8,128)S(1)} %copy.6.v_ref, f32[1,128,128]{2,1,0:T(8,128)S(1)} %copy-done.1), custom_call_target="tpu_custom_call" | custom-call | flops 125829120 | bytes 655360 | tf_op jit(solution)/shard_map/chase/pallas_call | solution.py:357
  49.5 0.7 %constant_dynamic-slice_fusion = f32[256,128]{1,0:T(8,128)} fusion(f32[384,128]{1,0:T(8,128)S(1)} %chase.1, s32[]{:T(128)S(6)} %select_n.3), kind=kLoop, calls=%fused_computation | loop fusion | bytes 262148 | tf_op jit(solution)/shard_map/dynamic_slice | solution.py:400
Async XLA Ops:
  0.7 1.0 %copy-start = (f32[256,128]{1,0:T(8,128)S(1)}, f32[256,128]{1,0:T(8,128)}, u32[]{:S(2)}) copy-start(f32[256,128]{1,0:T(8,128)} %e_ref.1) | copy-start | bytes 393220
  0.7 1.0 %copy-start.1 = (f32[1,128,128]{2,1,0:T(8,128)S(1)}, f32[1,128,128]{2,1,0:T(8,128)}, u32[]{:S(2)}) copy-start(f32[1,128,128]{2,1,0:T(8,128)} %t_ref.1) | copy-start | bytes 196612
  0.7 1.0 %copy-start.2 = (s32[1,30]{1,0:T(1,128)S(1)}, s32[1,30]{1,0:T(1,128)}, u32[]{:S(2)}) copy-start(s32[1,30]{1,0:T(1,128)} %plan_ref.1) | copy-start | bytes 364

commit v3 on v2

--- a/solution.py
+++ b/solution.py
@@ -36,9 +36,11 @@
         start_z = (0.0, 0.9, 1.9, 2.8, 5.8, 6.7, 7.6, 8.4)
         start_y = (0.4, 2.2, 4.7, 3.3)
         start = {4 * z + y: start_z[z] + start_y[y] for z in range(8) for y in range(4)}
-        served = {(7, 0): (6, 0), (5, 1): (4, 1), (6, 1): (5, 0), (7, 1): (0, 1)}
-        for y in (2, 3):
-            served.update({(4 + k, y): (3 - k, y) for k in range(4)})
+        served = {
+            (7, 0): (1, 0), (5, 1): (4, 0), (6, 1): (3, 1), (7, 1): (0, 1),
+            (4, 2): (3, 2), (5, 2): (4, 1), (6, 2): (1, 2), (7, 2): (0, 2),
+            (4, 3): (3, 3), (5, 3): (5, 0), (6, 3): (6, 0), (7, 3): (0, 3),
+        }
         partner = {4 * a + b: 4 * d + e for (a, b), (d, e) in served.items()}
     else:
         start = {k: k for k in range(cols)}
@@ -48,8 +50,8 @@
 
 
 def kernel(
-    rows, cols, off_ref, plan_ref, e_ref, v_ref, t_ref, y_ref,
-    xin, vbuf, tbuf, mine, g1, stage, stage3, g2, g3, ebuf, p1buf, fbuf, abuf, hbuf, bbuf, pbuf, sbuf, cbuf, dbuf,
+    rows, cols, off_hbm, plan_hbm, e_ref, v_ref, t_ref, y_ref,
+    off_ref, plan_ref, xin, low, up, mine, g1, stage, g2, g3, ebuf, p1buf, fbuf, abuf, hbuf, bbuf, pbuf, sbuf, cbuf, dbuf,
     lsem, hsem, s1, s2, s3, psem, asem, bsend, brecv, dsem, qsem, rowsem,
 ):
     nb = t_ref.shape[1]
@@ -84,13 +86,24 @@
     def await_bytes(ref, sem):
         pltpu.make_async_copy(ref, ref, sem).wait()
 
-    vbuf[2 * nb - 1 : 2 * nb] = jnp.zeros((1, nb), F32)
-    get_v = pltpu.make_async_copy(v_ref.at[0], vbuf.at[pl.ds(0, 2 * nb - 1)], lsem.at[0])
-    get_t = pltpu.make_async_copy(t_ref.at[0], tbuf, lsem.at[1])
+    at = pl.multiple_of(r * part, part)
+    end = jnp.minimum(nb + at + part - 1, 2 * nb - 2)
+    get_low = pltpu.make_async_copy(v_ref.at[pl.ds(at, part), 0], low, lsem.at[0])
+    get_up = pltpu.make_async_copy(
+        v_ref.at[pl.ds(nb + at, part - 1), 0], up.at[pl.ds(0, part - 1)], lsem.at[1]
+    )
+    get_end = pltpu.make_async_copy(
+        v_ref.at[pl.ds(end, 1), 0], up.at[pl.ds(part - 1, 1)], lsem.at[5]
+    )
+    get_t = pltpu.make_async_copy(
+        t_ref.at[0, pl.ds(at, part)], mine.at[pl.ds(part, part)], lsem.at[6]
+    )
+    mine_parts = (get_low, get_up, get_end, get_t)
     get_e = pltpu.make_async_copy(e_ref, xin.at[pl.ds(nb, own)], lsem.at[2])
-    get_v.start()
-    get_t.start()
-    get_e.start()
+    get_plan = pltpu.make_async_copy(plan_hbm, plan_ref, lsem.at[3])
+    get_off = pltpu.make_async_copy(off_hbm, off_ref, lsem.at[4])
+    for copy in mine_parts + (get_e, get_plan, get_off):
+        copy.start()
 
     barrier = pltpu.get_barrier_semaphore()
 
@@ -109,15 +122,11 @@
                 signal(barrier, row_at(k), other)
 
     xin[0:nb] = jnp.zeros((nb, nb), F32)
-    get_v.wait()
-    get_t.wait()
-    at = pl.multiple_of(r * part, part)
+    for copy in mine_parts:
+        copy.wait()
     row_ids = lax.broadcasted_iota(jnp.int32, (part, nb), 0) + at
     col_ids = lax.broadcasted_iota(jnp.int32, (part, nb), 1)
-    mine[0:part] = jnp.where(
-        row_ids >= col_ids, vbuf[pl.ds(at, part)], vbuf[pl.ds(nb + at, part)]
-    )
-    mine[part : 2 * part] = tbuf[pl.ds(at, part)]
+    mine[0:part] = jnp.where(row_ids >= col_ids, low[...], up[...])
 
     pl.semaphore_wait(barrier, len(early) + rows - 1 - is_early.astype(jnp.int32))
 
@@ -142,6 +151,9 @@
             signal(rowsem, row_at(k), other)
         await_bytes(g1, s1.at[1])
         head.start()
+
+    get_plan.wait()
+    get_off.wait()
 
     order = sorted(range(1, rows), key=lambda k: -min(k, rows - k)) + [0]
 
@@ -162,13 +174,6 @@
     def _():
         pl.semaphore_wait(rowsem, rows - 1)
         relay.start()
-
-    for k in order:
-        to = row_at(k)
-        dst = stage3.at[k] if k else g3.at[r]
-        dst[...] = pick(to, 2)
-        if k:
-            remote(stage3.at[k], g3.at[r], s3.at[0], s3.at[1], to, c).start()
 
     get_e.wait()
     head.wait_recv()
@@ -197,6 +202,11 @@
         return eye - w[:nb, :nb], -w[:nb, nb:], -w[nb:, :nb], fresh - w[nb:, nb:]
 
     await_bytes(g2.at[pl.ds(0, rows - 1)], s2.at[1])
+
+    third = remote(
+        g2.at[:, pl.ds(0, 2 * part)], g3, s3.at[0], s3.at[1], row_at(rows - 1), c
+    )
+    third.start()
     c0, d0, a0, b0 = block_map(0, g2[:, 0:part], g2[:, part : 2 * part])
     c1, d1, a1, b1 = block_map(1, g2[:, 2 * part : 3 * part], g2[:, 3 * part : 4 * part])
     w = mm(jnp.concatenate([a1, c1], axis=0), jnp.concatenate([a0, b0], axis=1))
@@ -226,7 +236,7 @@
         fbuf[1] = w[:, nb:] + ebuf[1]
         to_pair.start()
 
-    await_bytes(g3.at[pl.ds(0, rows - 1)], s3.at[1])
+    third.wait_recv()
     c2, d2 = block_map(2, g3[:, 0:part], g3[:, part : 2 * part])
     w = mm(c2, both(ebuf))
     cbuf[2 * nb : 3 * nb] = w[:, :nb]
@@ -309,7 +319,7 @@
     await_bytes(sent, s1.at[0])
     head.wait_send()
     await_bytes(g2.at[pl.ds(0, rows - 1)], s2.at[0])
-    await_bytes(g3.at[pl.ds(0, rows - 1)], s3.at[0])
+    third.wait_send()
 
     @pl.when(is_late)
     def _():
@@ -358,21 +368,22 @@
             functools.partial(kernel, rows, cols),
             out_shape=jax.ShapeDtypeStruct((3 * nb, width), F32),
             in_specs=[
-                pl.BlockSpec(memory_space=pltpu.SMEM),
-                pl.BlockSpec(memory_space=pltpu.SMEM),
-                pl.BlockSpec(memory_space=pltpu.HBM),
-                pl.BlockSpec(memory_space=pltpu.HBM),
-                pl.BlockSpec(memory_space=pltpu.HBM),
+                pl.BlockSpec(memory_space=pl.ANY),
+                pl.BlockSpec(memory_space=pl.ANY),
+                pl.BlockSpec(memory_space=pl.ANY),
+                pl.BlockSpec(memory_space=pl.ANY),
+                pl.BlockSpec(memory_space=pl.ANY),
             ],
             out_specs=pl.BlockSpec(memory_space=pltpu.VMEM),
             scratch_shapes=[
+                pltpu.SMEM(offsets.shape, jnp.int32),
+                pltpu.SMEM(plan.shape, jnp.int32),
                 pltpu.VMEM((nb + 2 * own, width), F32),
-                pltpu.VMEM((2 * nb, nb), F32),
-                pltpu.VMEM(square, F32),
+                pltpu.VMEM((part, nb), F32),
+                pltpu.VMEM((part, nb), F32),
                 pltpu.VMEM((2 * part, nb), F32),
                 pltpu.VMEM((cols, 2 * part, nb), F32),
                 pltpu.VMEM((rows, 4 * part, nb), F32),
-                pltpu.VMEM((rows, 2 * part, nb), F32),
                 pltpu.VMEM((rows, 4 * part, nb), F32),
                 pltpu.VMEM((rows, 2 * part, nb), F32),
                 pltpu.VMEM((2,) + square, F32),
@@ -385,18 +396,18 @@
                 pltpu.VMEM(square, F32),
                 pltpu.VMEM((3 * nb, nb), F32),
                 pltpu.VMEM((3 * nb, width), F32),
-                dma((3,)), dma((2,)), dma((2,)), dma((2,)), dma((2,)), dma((2,)), dma((2,)),
+                dma((7,)), dma((2,)), dma((2,)), dma((2,)), dma((2,)), dma((2,)), dma((2,)),
                 dma((rows // 4, 2)), dma((rows // 4, 2)), dma((2,)), dma((1,)),
                 pltpu.SemaphoreType.REGULAR,
             ],
             compiler_params=pltpu.CompilerParams(
-                collective_id=0, has_side_effects=True, vmem_limit_bytes=24 * 2**20
+                collective_id=0, has_side_effects=True, vmem_limit_bytes=60 * 2**20
             ),
             cost_estimate=pl.CostEstimate(
                 flops=2 * 30 * nb**3, bytes_accessed=4 * 10 * nb * nb, transcendentals=0
             ),
             name="chase",
-        )(offsets, plan, eigvecs, refl_v, refl_t)
+        )(offsets, plan, eigvecs, refl_v.transpose(1, 0, 2), refl_t)
         return lax.dynamic_slice(y, (nb - offsets[0], 0), (own, width))
 
     return jax.shard_map(

time: 50.3 us -> 52.5 us (1.044)
  the two profiles are of different devices: /device:TPU:415 before, /device:TPU:359 now
where the time goes in v3:
time: 52.5 us; the launch traced here: 52.3 us
  Pallas kernels  50.1 us (95%)
  local copies, waits for them, and re-layouts  1.59 us (3%)
  between operations  0.67 us (1%)
    pallas_call x1, Pallas kernels, on_device(): pl.pallas_call(functools.partial(kernel, rows, cols), out_shape=jax.Shape...  50.1 us
    dynamic_slice x1, local copies, waits for them, and re-layouts, on_device(): return lax.dynamic_slice(y, (nb - offsets[0], 0), (own, width))  1.59 us

profile of v3, /device:TPU:359, one launch (start us, length us, event | category | flops | bytes accessed | tf_op | source)
XLA Modules:
  0.0 52.3 jit_solution(13138438698656575366)
XLA Ops:
  0.7 50.1 %chase.1 = f32[384,128]{1,0:T(8,128)} custom-call(s32[1]{0:T(128)S(6)} %copy.6.off_hbm, s32[1,30]{1,0:T(1,128)} %plan_hbm.1, f32[256,128]{1,0:T(8,128)} %e_ref.1, f32[255,1,128]{2,1,0:T(1,128)} %bitcast.3, f32[1,128,128]{2,1,0:T(8,128)} %t_ref.1), custom_call_target="tpu_custom_call" | custom-call | flops 125829120 | bytes 655360 | tf_op jit(solution)/shard_map/chase/pallas_call | solution.py:367
  50.7 1.6 %constant_dynamic-slice_fusion = f32[256,128]{1,0:T(8,128)} fusion(f32[384,128]{1,0:T(8,128)} %chase.1, s32[]{:T(128)S(6)} %select_n.3), kind=kLoop, calls=%fused_computation | loop fusion | bytes 262148 | tf_op jit(solution)/shard_map/dynamic_slice | solution.py:411

commit v4 on v3

--- a/solution.py
+++ b/solution.py
@@ -46,13 +46,14 @@
         start = {k: k for k in range(cols)}
         partner = {k: k - cols // 2 for k in range((cols + 1) // 2, cols)}
     order = sorted(start, key=lambda k: start[k])
-    return [k for k in order if k not in partner], partner
+    early = [k for k in order if k not in partner]
+    return early, [k for k in order if k in partner], partner
 
 
 def kernel(
     rows, cols, off_hbm, plan_hbm, e_ref, v_ref, t_ref, y_ref,
     off_ref, plan_ref, xin, low, up, mine, g1, stage, g2, g3, ebuf, p1buf, fbuf, abuf, hbuf, bbuf, pbuf, sbuf, cbuf, dbuf,
-    lsem, hsem, s1, s2, s3, psem, asem, bsend, brecv, dsem, qsem, rowsem,
+    lsem, hsem, s1, s2, s3, psem, asem, bsend, brecv, dsem, rowsem, gosem,
 ):
     nb = t_ref.shape[1]
     part = nb // rows
@@ -61,7 +62,7 @@
     c = lax.axis_index("col")
     core, pair, x = r % 2, (r // 2) % 2, r // 4
     groups = rows // 4
-    early, partner = classes(cols)
+    early, late, partner = classes(cols)
     blocks = 2 * rows - 2
 
     is_late = functools.reduce(jnp.logical_or, [c == k for k in partner])
@@ -130,50 +131,50 @@
 
     pl.semaphore_wait(barrier, len(early) + rows - 1 - is_early.astype(jnp.int32))
 
-    for k in early:
-        @pl.when(c != k)
-        def _(k=k):
-            remote(mine, g1.at[c], s1.at[0], s1.at[1], r, k).start()
-
+    def share(to, own_class):
+        for k in to:
+            @pl.when((c != k) & own_class)
+            def _(k=k):
+                remote(mine, g1.at[c], s1.at[0], s1.at[1], r, k).start()
+
+    share(early, True)
     head = remote(
         e_ref, xin.at[pl.ds(nb + own, own)], hsem.at[0], hsem.at[1], row_at(rows - 1), c
     )
+    got1 = g1.at[pl.ds(0, cols - 1)]
+    g1[c] = mine[...]
 
     @pl.when(is_early)
     def _():
         head.start()
-        g1[c] = mine[...]
-        await_bytes(g1.at[pl.ds(0, cols - 1)], s1.at[1])
+        await_bytes(got1, s1.at[1])
+
+        @pl.when(serves)
+        def _():
+            pl.semaphore_wait(rowsem, rows - 1)
+            signal(gosem, r, other)
 
     @pl.when(is_late)
     def _():
         for k in range(1, rows):
             signal(rowsem, row_at(k), other)
-        await_bytes(g1, s1.at[1])
+        pl.semaphore_wait(gosem, 1)
+        share(late, True)
         head.start()
+        await_bytes(got1, s1.at[1])
 
     get_plan.wait()
     get_off.wait()
 
     order = sorted(range(1, rows), key=lambda k: -min(k, rows - k)) + [0]
-
-    def pick(to, j):
-        return g1[plan_ref[0, jnp.clip(2 * to - 1 + j, 0, blocks - 1)]]
-
     for k in order:
-        to = row_at(k)
         dst = stage.at[k] if k else g2.at[r]
-        dst[0 : 2 * part] = pick(to, 0)
-        dst[2 * part : 4 * part] = pick(to, 1)
-        if k:
-            remote(stage.at[k], g2.at[r], s2.at[0], s2.at[1], to, c).start()
-
-    relay = remote(g1, g1, qsem.at[0], s1.at[1], r, other)
-
-    @pl.when(serves)
-    def _():
-        pl.semaphore_wait(rowsem, rows - 1)
-        relay.start()
+        for j in range(2):
+            block = jnp.clip(2 * row_at(k) - 1 + j, 0, blocks - 1)
+            dst[2 * part * j : 2 * part * (j + 1)] = g1[plan_ref[0, block]]
+    for k in order[:-1]:
+        remote(stage.at[k], g2.at[r], s2.at[0], s2.at[1], row_at(k), c).start()
+    share(late, is_early)
 
     get_e.wait()
     head.wait_recv()
@@ -315,19 +316,10 @@
 
     y_ref[...] = mm(cbuf[...], sbuf[...]) + dbuf[...]
 
-    sent = g1.at[pl.ds(0, len(early) - 1)]
-    await_bytes(sent, s1.at[0])
+    await_bytes(got1, s1.at[0])
     head.wait_send()
     await_bytes(g2.at[pl.ds(0, rows - 1)], s2.at[0])
     third.wait_send()
-
-    @pl.when(is_late)
-    def _():
-        await_bytes(g1.at[0], s1.at[0])
-
-    @pl.when(serves)
-    def _():
-        relay.wait_send()
 
     @pl.when(core0)
     def _():
@@ -366,7 +358,7 @@
         square = (nb, nb)
         y = pl.pallas_call(
             functools.partial(kernel, rows, cols),
-            out_shape=jax.ShapeDtypeStruct((3 * nb, width), F32),
+            out_shape=pltpu.VMEM((3 * nb, width), F32),
             in_specs=[
                 pl.BlockSpec(memory_space=pl.ANY),
                 pl.BlockSpec(memory_space=pl.ANY),
@@ -397,8 +389,8 @@
                 pltpu.VMEM((3 * nb, nb), F32),
                 pltpu.VMEM((3 * nb, width), F32),
                 dma((7,)), dma((2,)), dma((2,)), dma((2,)), dma((2,)), dma((2,)), dma((2,)),
-                dma((rows // 4, 2)), dma((rows // 4, 2)), dma((2,)), dma((1,)),
-                pltpu.SemaphoreType.REGULAR,
+                dma((rows // 4, 2)), dma((rows // 4, 2)), dma((2,)),
+                pltpu.SemaphoreType.REGULAR, pltpu.SemaphoreType.REGULAR,
             ],
             compiler_params=pltpu.CompilerParams(
                 collective_id=0, has_side_effects=True, vmem_limit_bytes=60 * 2**20

time: 52.5 us -> 42.2 us (0.80)
  the two profiles are of different devices: /device:TPU:359 before, /device:TPU:455 now
where the time goes in v4:
time: 42.2 us; the launch traced here: 42 us
  Pallas kernels  40.7 us (96%)
  local copies, waits for them, and re-layouts  0.68 us (2%)
  between operations  0.67 us (2%)
    pallas_call x1, Pallas kernels, on_device(): pl.pallas_call(functools.partial(kernel, rows, cols), out_shape=pltpu.VME...  40.7 us

profile of v4, /device:TPU:455, one launch (start us, length us, event | category | flops | bytes accessed | tf_op | source)
XLA Modules:
  0.0 42.0 jit_solution(8680580255754113082)
XLA Ops:
  0.7 40.7 %chase.1 = f32[384,128]{1,0:T(8,128)S(1)} custom-call(s32[1]{0:T(128)S(6)} %copy.6.off_hbm, s32[1,30]{1,0:T(1,128)} %plan_hbm.1, f32[256,128]{1,0:T(8,128)} %e_ref.1, f32[255,1,128]{2,1,0:T(1,128)} %bitcast.3, f32[1,128,128]{2,1,0:T(8,128)} %t_ref.1), custom_call_target="tpu_custom_call" | custom-call | flops 125829120 | bytes 655360 | tf_op jit(solution)/shard_map/chase/pallas_call | solution.py:359
  41.4 0.7 %constant_dynamic-slice_fusion = f32[256,128]{1,0:T(8,128)} fusion(f32[384,128]{1,0:T(8,128)S(1)} %chase.1, s32[]{:T(128)S(6)} %select_n.3), kind=kLoop, calls=%fused_computation | loop fusion | bytes 262148 | tf_op jit(solution)/shard_map/dynamic_slice | solution.py:403

commit v5 on v4

--- a/solution.py
+++ b/solution.py
@@ -36,11 +36,9 @@
         start_z = (0.0, 0.9, 1.9, 2.8, 5.8, 6.7, 7.6, 8.4)
         start_y = (0.4, 2.2, 4.7, 3.3)
         start = {4 * z + y: start_z[z] + start_y[y] for z in range(8) for y in range(4)}
-        served = {
-            (7, 0): (1, 0), (5, 1): (4, 0), (6, 1): (3, 1), (7, 1): (0, 1),
-            (4, 2): (3, 2), (5, 2): (4, 1), (6, 2): (1, 2), (7, 2): (0, 2),
-            (4, 3): (3, 3), (5, 3): (5, 0), (6, 3): (6, 0), (7, 3): (0, 3),
-        }
+        served = {(7, 0): (6, 0), (5, 1): (4, 1), (6, 1): (3, 1), (7, 1): (0, 1)}
+        for y in (2, 3):
+            served.update({(4 + k, y): (3 - k, y) for k in range(4)})
         partner = {4 * a + b: 4 * d + e for (a, b), (d, e) in served.items()}
     else:
         start = {k: k for k in range(cols)}
@@ -53,7 +51,7 @@
 def kernel(
     rows, cols, off_hbm, plan_hbm, e_ref, v_ref, t_ref, y_ref,
     off_ref, plan_ref, xin, low, up, mine, g1, stage, g2, g3, ebuf, p1buf, fbuf, abuf, hbuf, bbuf, pbuf, sbuf, cbuf, dbuf,
-    lsem, hsem, s1, s2, s3, psem, asem, bsend, brecv, dsem, rowsem, gosem,
+    lsem, msem, hsem, s1, s2, s3, psem, asem, bsend, brecv, dsem, rowsem, colsem, gosem,
 ):
     nb = t_ref.shape[1]
     part = nb // rows
@@ -75,6 +73,14 @@
     def row_at(k):
         return lax.rem(r + k, rows)
 
+    swaps = cols % 8 == 0
+
+    def across(k):
+        return (lax.rem(c - k + 4 * cols, 4) == 2).astype(jnp.int32) if swaps else 0
+
+    def row_for(k):
+        return r ^ (2 * across(k))
+
     def remote(src, dst, send, recv, to_row, to_col):
         return pltpu.make_async_remote_copy(
             src_ref=src, dst_ref=dst, send_sem=send, recv_sem=recv,
@@ -87,33 +93,38 @@
     def await_bytes(ref, sem):
         pltpu.make_async_copy(ref, ref, sem).wait()
 
-    at = pl.multiple_of(r * part, part)
-    end = jnp.minimum(nb + at + part - 1, 2 * nb - 2)
-    get_low = pltpu.make_async_copy(v_ref.at[pl.ds(at, part), 0], low, lsem.at[0])
-    get_up = pltpu.make_async_copy(
-        v_ref.at[pl.ds(nb + at, part - 1), 0], up.at[pl.ds(0, part - 1)], lsem.at[1]
-    )
-    get_end = pltpu.make_async_copy(
-        v_ref.at[pl.ds(end, 1), 0], up.at[pl.ds(part - 1, 1)], lsem.at[5]
-    )
-    get_t = pltpu.make_async_copy(
-        t_ref.at[0, pl.ds(at, part)], mine.at[pl.ds(part, part)], lsem.at[6]
-    )
-    mine_parts = (get_low, get_up, get_end, get_t)
-    get_e = pltpu.make_async_copy(e_ref, xin.at[pl.ds(nb, own)], lsem.at[2])
-    get_plan = pltpu.make_async_copy(plan_hbm, plan_ref, lsem.at[3])
-    get_off = pltpu.make_async_copy(off_hbm, off_ref, lsem.at[4])
-    for copy in mine_parts + (get_e, get_plan, get_off):
+    mine_parts = []
+    for i in range(1 + swaps):
+        at = pl.multiple_of((r ^ (2 * i)) * part, part)
+        end = jnp.minimum(nb + at + part - 1, 2 * nb - 2)
+        mine_parts += [
+            pltpu.make_async_copy(v_ref.at[pl.ds(at, part), 0], low.at[i], msem.at[i, 0]),
+            pltpu.make_async_copy(
+                v_ref.at[pl.ds(nb + at, part - 1), 0],
+                up.at[i, pl.ds(0, part - 1)],
+                msem.at[i, 1],
+            ),
+            pltpu.make_async_copy(
+                v_ref.at[pl.ds(end, 1), 0], up.at[i, pl.ds(part - 1, 1)], msem.at[i, 2]
+            ),
+            pltpu.make_async_copy(
+                t_ref.at[0, pl.ds(at, part)], mine.at[i, pl.ds(part, part)], msem.at[i, 3]
+            ),
+        ]
+    get_e = pltpu.make_async_copy(e_ref, xin.at[pl.ds(nb, own)], lsem.at[0])
+    get_plan = pltpu.make_async_copy(plan_hbm, plan_ref, lsem.at[1])
+    get_off = pltpu.make_async_copy(off_hbm, off_ref, lsem.at[2])
+    for copy in mine_parts + [get_e, get_plan, get_off]:
         copy.start()
 
     barrier = pltpu.get_barrier_semaphore()
 
     @pl.when(is_early)
     def _():
-        for k in list(partner) + early[::-1]:
+        for k in late[::-1] + early[::-1]:
             @pl.when(c != k)
             def _(k=k):
-                signal(barrier, r, k)
+                signal(barrier, row_for(k), k)
         for k in range(1, rows):
             signal(barrier, row_at(k), c)
 
@@ -121,48 +132,62 @@
         def _():
             for k in range(1, rows):
                 signal(barrier, row_at(k), other)
+
+    @pl.when(is_late)
+    def _():
+        pl.semaphore_wait(barrier, len(early) + rows - 1)
+        for k in early:
+            signal(colsem, row_for(k), k)
+        for k in range(1, rows):
+            signal(rowsem, row_at(k), other)
 
     xin[0:nb] = jnp.zeros((nb, nb), F32)
     for copy in mine_parts:
         copy.wait()
-    row_ids = lax.broadcasted_iota(jnp.int32, (part, nb), 0) + at
-    col_ids = lax.broadcasted_iota(jnp.int32, (part, nb), 1)
-    mine[0:part] = jnp.where(row_ids >= col_ids, low[...], up[...])
-
-    pl.semaphore_wait(barrier, len(early) + rows - 1 - is_early.astype(jnp.int32))
-
-    def share(to, own_class):
+    for i in range(1 + swaps):
+        at = (r ^ (2 * i)) * part
+        row_ids = lax.broadcasted_iota(jnp.int32, (part, nb), 0) + at
+        col_ids = lax.broadcasted_iota(jnp.int32, (part, nb), 1)
+        mine[i, 0:part] = jnp.where(row_ids >= col_ids, low[i], up[i])
+
+    @pl.when(is_early)
+    def _():
+        pl.semaphore_wait(barrier, len(early) - 1 + rows - 1)
+
+    def share(to):
         for k in to:
-            @pl.when((c != k) & own_class)
+            @pl.when(c != k)
             def _(k=k):
-                remote(mine, g1.at[c], s1.at[0], s1.at[1], r, k).start()
-
-    share(early, True)
+                remote(
+                    mine.at[across(k)], g1.at[c], s1.at[0], s1.at[1], row_for(k), k
+                ).start()
+
+    share(early)
     head = remote(
         e_ref, xin.at[pl.ds(nb + own, own)], hsem.at[0], hsem.at[1], row_at(rows - 1), c
     )
     got1 = g1.at[pl.ds(0, cols - 1)]
-    g1[c] = mine[...]
+    g1[c] = mine[0]
 
     @pl.when(is_early)
     def _():
         head.start()
-        await_bytes(got1, s1.at[1])
+        pl.semaphore_wait(colsem, len(late))
 
         @pl.when(serves)
         def _():
             pl.semaphore_wait(rowsem, rows - 1)
             signal(gosem, r, other)
 
+        share(late)
+
     @pl.when(is_late)
     def _():
-        for k in range(1, rows):
-            signal(rowsem, row_at(k), other)
         pl.semaphore_wait(gosem, 1)
-        share(late, True)
+        share(late)
         head.start()
-        await_bytes(got1, s1.at[1])
-
+
+    await_bytes(got1, s1.at[1])
     get_plan.wait()
     get_off.wait()
 
@@ -174,7 +199,6 @@
             dst[2 * part * j : 2 * part * (j + 1)] = g1[plan_ref[0, block]]
     for k in order[:-1]:
         remote(stage.at[k], g2.at[r], s2.at[0], s2.at[1], row_at(k), c).start()
-    share(late, is_early)
 
     get_e.wait()
     head.wait_recv()
@@ -371,9 +395,9 @@
                 pltpu.SMEM(offsets.shape, jnp.int32),
                 pltpu.SMEM(plan.shape, jnp.int32),
                 pltpu.VMEM((nb + 2 * own, width), F32),
-                pltpu.VMEM((part, nb), F32),
-                pltpu.VMEM((part, nb), F32),
-                pltpu.VMEM((2 * part, nb), F32),
+                pltpu.VMEM((2, part, nb), F32),
+                pltpu.VMEM((2, part, nb), F32),
+                pltpu.VMEM((2, 2 * part, nb), F32),
                 pltpu.VMEM((cols, 2 * part, nb), F32),
                 pltpu.VMEM((rows, 4 * part, nb), F32),
                 pltpu.VMEM((rows, 4 * part, nb), F32),
@@ -388,9 +412,10 @@
                 pltpu.VMEM(square, F32),
                 pltpu.VMEM((3 * nb, nb), F32),
                 pltpu.VMEM((3 * nb, width), F32),
-                dma((7,)), dma((2,)), dma((2,)), dma((2,)), dma((2,)), dma((2,)), dma((2,)),
+                dma((3,)), dma((2, 4)), dma((2,)), dma((2,)), dma((2,)), dma((2,)), dma((2,)), dma((2,)),
                 dma((rows // 4, 2)), dma((rows // 4, 2)), dma((2,)),
                 pltpu.SemaphoreType.REGULAR, pltpu.SemaphoreType.REGULAR,
+                pltpu.SemaphoreType.REGULAR,
             ],
             compiler_params=pltpu.CompilerParams(
                 collective_id=0, has_side_effects=True, vmem_limit_bytes=60 * 2**20

time: 42.2 us -> 38.5 us (0.912)
  the two profiles are of different devices: /device:TPU:455 before, /device:TPU:7 now
where the time goes in v5:
time: 38.5 us; the launch traced here: 38.4 us
  Pallas kernels  37.1 us (96%)
  local copies, waits for them, and re-layouts  0.68 us (2%)
  between operations  0.67 us (2%)
    pallas_call x1, Pallas kernels, on_device(): pl.pallas_call(functools.partial(kernel, rows, cols), out_shape=pltpu.VME...  37.1 us

profile of v5, /device:TPU:7, one launch (start us, length us, event | category | flops | bytes accessed | tf_op | source)
XLA Modules:
  0.0 38.4 jit_solution(4474969476344481243)
XLA Ops:
  0.7 37.1 %chase.1 = f32[384,128]{1,0:T(8,128)S(1)} custom-call(s32[1]{0:T(128)S(6)} %copy.6.off_hbm, s32[1,30]{1,0:T(1,128)} %plan_hbm.1, f32[256,128]{1,0:T(8,128)} %e_ref.1, f32[255,1,128]{2,1,0:T(1,128)} %bitcast.3, f32[1,128,128]{2,1,0:T(8,128)} %t_ref.1), custom_call_target="tpu_custom_call" | custom-call | flops 125829120 | bytes 655360 | tf_op jit(solution)/shard_map/chase/pallas_call | solution.py:383
  37.7 0.7 %constant_dynamic-slice_fusion = f32[256,128]{1,0:T(8,128)} fusion(f32[384,128]{1,0:T(8,128)S(1)} %chase.1, s32[]{:T(128)S(6)} %select_n.3), kind=kLoop, calls=%fused_computation | loop fusion | bytes 262148 | tf_op jit(solution)/shard_map/dynamic_slice | solution.py:428

commit v6 on v5

--- a/solution.py
+++ b/solution.py
@@ -36,9 +36,10 @@
         start_z = (0.0, 0.9, 1.9, 2.8, 5.8, 6.7, 7.6, 8.4)
         start_y = (0.4, 2.2, 4.7, 3.3)
         start = {4 * z + y: start_z[z] + start_y[y] for z in range(8) for y in range(4)}
-        served = {(7, 0): (6, 0), (5, 1): (4, 1), (6, 1): (3, 1), (7, 1): (0, 1)}
-        for y in (2, 3):
+        served = {(5, 0): (4, 0), (6, 0): (3, 0), (7, 0): (1, 0), (3, 2): (2, 2)}
+        for y in (1, 2, 3):
             served.update({(4 + k, y): (3 - k, y) for k in range(4)})
+        served[4, 2] = (2, 2)
         partner = {4 * a + b: 4 * d + e for (a, b), (d, e) in served.items()}
     else:
         start = {k: k for k in range(cols)}
@@ -63,11 +64,8 @@
     early, late, partner = classes(cols)
     blocks = 2 * rows - 2
 
-    is_late = functools.reduce(jnp.logical_or, [c == k for k in partner])
-    serves = functools.reduce(jnp.logical_or, [c == k for k in partner.values()])
-    other = sum(
-        jnp.where(c == a, b, 0) + jnp.where(c == b, a, 0) for a, b in partner.items()
-    )
+    is_late = functools.reduce(jnp.logical_or, [c == k for k in late])
+    server = sum(jnp.where(c == a, b, 0) for a, b in partner.items())
     is_early = jnp.logical_not(is_late)
 
     def row_at(k):
@@ -114,7 +112,7 @@
     get_e = pltpu.make_async_copy(e_ref, xin.at[pl.ds(nb, own)], lsem.at[0])
     get_plan = pltpu.make_async_copy(plan_hbm, plan_ref, lsem.at[1])
     get_off = pltpu.make_async_copy(off_hbm, off_ref, lsem.at[2])
-    for copy in mine_parts + [get_e, get_plan, get_off]:
+    for copy in mine_parts:
         copy.start()
 
     barrier = pltpu.get_barrier_semaphore()
@@ -128,10 +126,11 @@
         for k in range(1, rows):
             signal(barrier, row_at(k), c)
 
-        @pl.when(serves)
-        def _():
-            for k in range(1, rows):
-                signal(barrier, row_at(k), other)
+        for a, b in partner.items():
+            @pl.when(c == b)
+            def _(a=a):
+                for k in range(1, rows):
+                    signal(barrier, row_at(k), a)
 
     @pl.when(is_late)
     def _():
@@ -139,7 +138,7 @@
         for k in early:
             signal(colsem, row_for(k), k)
         for k in range(1, rows):
-            signal(rowsem, row_at(k), other)
+            signal(rowsem, row_at(k), server)
 
     xin[0:nb] = jnp.zeros((nb, nb), F32)
     for copy in mine_parts:
@@ -163,6 +162,8 @@
                 ).start()
 
     share(early)
+    for copy in (get_e, get_plan, get_off):
+        copy.start()
     head = remote(
         e_ref, xin.at[pl.ds(nb + own, own)], hsem.at[0], hsem.at[1], row_at(rows - 1), c
     )
@@ -173,11 +174,14 @@
     def _():
         head.start()
         pl.semaphore_wait(colsem, len(late))
-
-        @pl.when(serves)
-        def _():
-            pl.semaphore_wait(rowsem, rows - 1)
-            signal(gosem, r, other)
+        for b in sorted(set(partner.values())):
+            served = [k for k in late if partner[k] == b]
+
+            @pl.when(c == b)
+            def _(served=served):
+                pl.semaphore_wait(rowsem, (rows - 1) * len(served))
+                for a in served:
+                    signal(gosem, r, a)
 
         share(late)
 
@@ -261,12 +265,6 @@
         fbuf[1] = w[:, nb:] + ebuf[1]
         to_pair.start()
 
-    third.wait_recv()
-    c2, d2 = block_map(2, g3[:, 0:part], g3[:, part : 2 * part])
-    w = mm(c2, both(ebuf))
-    cbuf[2 * nb : 3 * nb] = w[:, :nb]
-    dbuf[2 * nb : 3 * nb] = w[:, nb:] + d2
-
     def along_x(step, half):
         return remote(
             hbuf.at[half], bbuf.at[x, half], bsend.at[step, half], brecv.at[x, half],
@@ -297,15 +295,21 @@
                 def _():
                     along_x(step, 0).start()
 
-        @pl.when(pair == 0)
-        def _():
-            pbuf[...] = p1buf[...]
-
-        @pl.when(pair == 1)
-        def _():
-            w = mm(p1buf[0], both(abuf))
-            pbuf[0] = w[:, :nb]
-            pbuf[1] = w[:, nb:] + p1buf[1]
+    third.wait_recv()
+    c2, d2 = block_map(2, g3[:, 0:part], g3[:, part : 2 * part])
+    w = mm(c2, both(ebuf))
+    cbuf[2 * nb : 3 * nb] = w[:, :nb]
+    dbuf[2 * nb : 3 * nb] = w[:, nb:] + d2
+
+    @pl.when(core1 & (pair == 0))
+    def _():
+        pbuf[...] = p1buf[...]
+
+    @pl.when(core1 & (pair == 1))
+    def _():
+        w = mm(p1buf[0], both(abuf))
+        pbuf[0] = w[:, :nb]
+        pbuf[1] = w[:, nb:] + p1buf[1]
 
     @pl.when(core0 & (pair == 1))
     def _():
@@ -338,7 +342,8 @@
     def _():
         state.wait_recv()
 
-    y_ref[...] = mm(cbuf[...], sbuf[...]) + dbuf[...]
+    dbuf[...] = mm(cbuf[...], sbuf[...]) + dbuf[...]
+    y_ref[...] = dbuf[pl.ds(nb - off, own)]
 
     await_bytes(got1, s1.at[0])
     head.wait_send()
@@ -382,7 +387,7 @@
         square = (nb, nb)
         y = pl.pallas_call(
             functools.partial(kernel, rows, cols),
-            out_shape=pltpu.VMEM((3 * nb, width), F32),
+            out_shape=pltpu.VMEM((own, width), F32),
             in_specs=[
                 pl.BlockSpec(memory_space=pl.ANY),
                 pl.BlockSpec(memory_space=pl.ANY),
@@ -425,7 +430,7 @@
             ),
             name="chase",
         )(offsets, plan, eigvecs, refl_v.transpose(1, 0, 2), refl_t)
-        return lax.dynamic_slice(y, (nb - offsets[0], 0), (own, width))
+        return y
 
     return jax.shard_map(
         on_device,

time: 38.5 us -> 37.9 us (0.984)
  Pallas kernels: 37.1 us -> 36.4 us
    pallas_call x1, Pallas kernels: 37.1 us -> 36.4 us  [on_device(): pl.pallas_call(functools.partial(kernel, rows, cols), out_shape=pltpu.VME...]
    dynamic_slice x1 -> x0, local copies, waits for them, and re-layouts: 0.68 us -> none  [on_device(): return lax.dynamic_slice(y, (nb - offsets[0], 0), (own, width))]
    unnamed x0 -> x1, local copies, waits for them, and re-layouts: none -> 0.66 us
where the time goes in v6:
time: 37.9 us; the launch traced here: 37.7 us
  Pallas kernels  36.4 us (96%)
  local copies, waits for them, and re-layouts  0.66 us (2%)
  between operations  0.66 us (2%)
    pallas_call x1, Pallas kernels, on_device(): pl.pallas_call(functools.partial(kernel, rows, cols), out_shape=pltpu.VME...  36.4 us

profile of v6, /device:TPU:7, one launch (start us, length us, event | category | flops | bytes accessed | tf_op | source)
XLA Modules:
  0.0 37.7 jit_solution(5765349555646957133)
XLA Ops:
  0.7 36.4 %chase.1 = f32[256,128]{1,0:T(8,128)S(1)} custom-call(s32[1]{0:T(128)S(6)} %copy.8.off_hbm, s32[1,30]{1,0:T(1,128)} %plan_hbm.1, f32[256,128]{1,0:T(8,128)} %e_ref.1, f32[255,1,128]{2,1,0:T(1,128)} %bitcast.1, f32[1,128,128]{2,1,0:T(8,128)} %t_ref.1), custom_call_target="tpu_custom_call" | custom-call | flops 125829120 | bytes 655360 | tf_op jit(solution)/shard_map/chase/pallas_call | solution.py:388
  37.0 0.7 %copy.7 = f32[256,128]{1,0:T(8,128)} copy(f32[256,128]{1,0:T(8,128)S(1)} %chase.1) | data formatting | bytes 262144

commit v7 on v6

--- a/solution.py
+++ b/solution.py
@@ -52,7 +52,7 @@
 def kernel(
     rows, cols, off_hbm, plan_hbm, e_ref, v_ref, t_ref, y_ref,
     off_ref, plan_ref, xin, low, up, mine, g1, stage, g2, g3, ebuf, p1buf, fbuf, abuf, hbuf, bbuf, pbuf, sbuf, cbuf, dbuf,
-    lsem, msem, hsem, s1, s2, s3, psem, asem, bsend, brecv, dsem, rowsem, colsem, gosem,
+    lsem, msem, hsem, s1, s2, s3, esem, psem, asem, bsend, brecv, dsem, rowsem, colsem, gosem,
 ):
     nb = t_ref.shape[1]
     part = nb // rows
@@ -109,7 +109,7 @@
                 t_ref.at[0, pl.ds(at, part)], mine.at[i, pl.ds(part, part)], msem.at[i, 3]
             ),
         ]
-    get_e = pltpu.make_async_copy(e_ref, xin.at[pl.ds(nb, own)], lsem.at[0])
+    get_e = pltpu.make_async_copy(e_ref, xin.at[pl.ds(own, own)], lsem.at[0])
     get_plan = pltpu.make_async_copy(plan_hbm, plan_ref, lsem.at[1])
     get_off = pltpu.make_async_copy(off_hbm, off_ref, lsem.at[2])
     for copy in mine_parts:
@@ -140,7 +140,10 @@
         for k in range(1, rows):
             signal(rowsem, row_at(k), server)
 
-    xin[0:nb] = jnp.zeros((nb, nb), F32)
+    @pl.when(core == 0)
+    def _():
+        xin[own - nb : own] = jnp.zeros((nb, nb), F32)
+
     for copy in mine_parts:
         copy.wait()
     for i in range(1 + swaps):
@@ -165,14 +168,23 @@
     for copy in (get_e, get_plan, get_off):
         copy.start()
     head = remote(
-        e_ref, xin.at[pl.ds(nb + own, own)], hsem.at[0], hsem.at[1], row_at(rows - 1), c
+        e_ref, xin.at[pl.ds(2 * own, own)], hsem.at[0], hsem.at[1], row_at(rows - 1), c
     )
+    tail = remote(e_ref, xin.at[pl.ds(0, own)], hsem.at[2], hsem.at[3], r ^ 1, c)
+
+    def send_rows():
+        head.start()
+
+        @pl.when(core == 0)
+        def _():
+            tail.start()
+
     got1 = g1.at[pl.ds(0, cols - 1)]
     g1[c] = mine[0]
 
     @pl.when(is_early)
     def _():
-        head.start()
+        send_rows()
         pl.semaphore_wait(colsem, len(late))
         for b in sorted(set(partner.values())):
             served = [k for k in late if partner[k] == b]
@@ -189,81 +201,124 @@
     def _():
         pl.semaphore_wait(gosem, 1)
         share(late)
-        head.start()
+        send_rows()
 
     await_bytes(got1, s1.at[1])
     get_plan.wait()
     get_off.wait()
 
-    order = sorted(range(1, rows), key=lambda k: -min(k, rows - k)) + [0]
+    chips = rows // 2
+    chip = r // 2
+    core0, core1 = core == 0, core == 1
+    order = sorted(range(1, chips), key=lambda k: -min(k, chips - k)) + [0]
+
+    def to_chip(k):
+        to = 2 * lax.rem(chip + k, chips) + 1
+        return remote(stage.at[k], g2.at[r], s2.at[0], s2.at[1], to, c)
+
     for k in order:
-        dst = stage.at[k] if k else g2.at[r]
-        for j in range(2):
-            block = jnp.clip(2 * row_at(k) - 1 + j, 0, blocks - 1)
-            dst[2 * part * j : 2 * part * (j + 1)] = g1[plan_ref[0, block]]
+        for j in range(4):
+            block = jnp.clip(4 * lax.rem(chip + k, chips) - 1 + j, 0, blocks - 1)
+            stage[k, 2 * part * j : 2 * part * (j + 1)] = g1[plan_ref[0, block]]
     for k in order[:-1]:
-        remote(stage.at[k], g2.at[r], s2.at[0], s2.at[1], row_at(k), c).start()
+        to_chip(k).start()
+
+    @pl.when(core0)
+    def _():
+        to_chip(0).start()
+
+    @pl.when(core1)
+    def _():
+        g2[r] = stage[0]
+        tail.wait_recv()
 
     get_e.wait()
     head.wait_recv()
     off = off_ref[0]
-    s0 = xin[pl.ds(off, nb)]
+    s0 = xin[pl.ds(off + own - nb, nb)]
 
     ri = lax.broadcasted_iota(jnp.int32, (nb, nb), 0)
     ci = lax.broadcasted_iota(jnp.int32, (nb, nb), 1)
     eye = (ri == ci).astype(F32)
 
-    def block_map(j, packed, factor):
-        number = 2 * r - 1 + j
-        live = ((number >= 0) & (number < blocks)).astype(F32)
-        fresh = xin[pl.ds(off + nb * (1 + j), nb)]
+    def triangles(packed):
         packed = packed.reshape(nb, nb)
-        factor = factor.reshape(nb, nb) * live
-        lower = jnp.where(ri >= ci, packed, 0.0)
-        upper = jnp.where(ri >= ci, 0.0, packed)
-        vectors = jnp.concatenate([lower, upper], axis=0)
-        tv = mm(factor, vectors, rhs_t=True)
-        m, n = tv[:, :nb], tv[:, nb:]
-        z = mm(n, fresh)
-        w = mm(vectors if j < 2 else lower, jnp.concatenate([m, z], axis=1))
-        if j == 2:
-            return eye - w[:, :nb], -w[:, nb:]
-        return eye - w[:nb, :nb], -w[:nb, nb:], -w[nb:, :nb], fresh - w[nb:, nb:]
-
-    await_bytes(g2.at[pl.ds(0, rows - 1)], s2.at[1])
-
+        return jnp.where(ri >= ci, packed, 0.0), jnp.where(ri >= ci, 0.0, packed)
+
+    def fresh(n):
+        return xin[pl.ds(off + own + nb * (n + 1), nb)]
+
+    def entry(j):
+        lo = 2 * part * j
+        return g2[:, lo : lo + part], g2[:, lo + part : lo + 2 * part]
+
+    def middle(n, packed, factor):
+        live = ((2 * r + n >= 0) & (2 * r + n < blocks)).astype(F32)
+        vectors = jnp.concatenate(triangles(packed), axis=0)
+        tv = mm(factor.reshape(nb, nb) * live, vectors, rhs_t=True)
+        return jnp.concatenate([tv[:, :nb], mm(tv[:, nb:], fresh(n))], axis=1)
+
+    def passed(n, packed, mid):
+        w = mm(triangles(packed)[1], mid)
+        return -w[:, :nb], fresh(n) - w[:, nb:]
+
+    def done(packed, mid):
+        w = mm(triangles(packed)[0], mid)
+        return eye - w[:, :nb], -w[:, nb:]
+
+    entries = remote(
+        g2.at[:, pl.ds(0, 6 * part)], g2.at[:, pl.ds(0, 6 * part)],
+        esem.at[0], esem.at[1], r ^ 1, c,
+    )
     third = remote(
-        g2.at[:, pl.ds(0, 2 * part)], g3, s3.at[0], s3.at[1], row_at(rows - 1), c
+        g2.at[:, pl.ds(0, 2 * part)], g3, s3.at[0], s3.at[1], row_at(rows - 2), c
     )
-    third.start()
-    c0, d0, a0, b0 = block_map(0, g2[:, 0:part], g2[:, part : 2 * part])
-    c1, d1, a1, b1 = block_map(1, g2[:, 2 * part : 3 * part], g2[:, 3 * part : 4 * part])
-    w = mm(jnp.concatenate([a1, c1], axis=0), jnp.concatenate([a0, b0], axis=1))
-    ebuf[0] = w[:nb, :nb]
-    ebuf[1] = w[:nb, nb:] + b1
-
-    to_core1 = remote(ebuf, p1buf, psem.at[0], psem.at[1], r ^ 1, c)
     to_pair = remote(fbuf, abuf, asem.at[0], asem.at[1], r ^ 2, c)
     prefix = remote(abuf, pbuf, psem.at[0], psem.at[1], r ^ 1, c)
     state = remote(sbuf, sbuf, dsem.at[0], dsem.at[1], r ^ 1, c)
-    core0, core1 = core == 0, core == 1
-
-    @pl.when(core0)
-    def _():
-        to_core1.start()
-
-    cbuf[0:nb] = c0
-    dbuf[0:nb] = d0
-    cbuf[nb : 2 * nb] = w[nb:, :nb]
-    dbuf[nb : 2 * nb] = w[nb:, nb:] + d1
 
     @pl.when(core1)
     def _():
-        to_core1.wait_recv()
+        await_bytes(g2.at[pl.ds(0, rows - 1)], s2.at[1])
+        entries.start()
+        mids = [middle(j - 3, *entry(j)) for j in range(4)]
+        (a0, b0), (a1, b1), (a2, b2), (a3, b3) = [
+            passed(j - 3, entry(j)[0], mids[j]) for j in range(4)
+        ]
+        first = mm(a1, jnp.concatenate([a0, b0], axis=1))
+        p1buf[0] = first[:, :nb]
+        p1buf[1] = first[:, nb:] + b1
+        second = mm(a3, jnp.concatenate([a2, b2], axis=1))
+        ebuf[0] = second[:, :nb]
+        ebuf[1] = second[:, nb:] + b3
         w = mm(ebuf[0], both(p1buf))
         fbuf[0] = w[:, :nb]
         fbuf[1] = w[:, nb:] + ebuf[1]
         to_pair.start()
+        third.start()
+        c2, d2 = done(entry(2)[0], mids[2])
+        cbuf[0:nb] = c2
+        dbuf[0:nb] = d2
+        c3, d3 = done(entry(3)[0], mids[3])
+        w = mm(c3, jnp.concatenate([a2, b2], axis=1))
+        cbuf[nb : 2 * nb] = w[:, :nb]
+        dbuf[nb : 2 * nb] = w[:, nb:] + d3
+
+    @pl.when(core0)
+    def _():
+        await_bytes(g2.at[:, pl.ds(0, 6 * part)], esem.at[1])
+        mids = [middle(j - 1, *entry(j)) for j in range(3)]
+        (a0, b0), (a1, b1) = [passed(j - 1, entry(j)[0], mids[j]) for j in range(2)]
+        (c0, d0), (c1, d1), (c2, d2) = [done(entry(j)[0], mids[j]) for j in range(3)]
+        cbuf[0:nb] = c0
+        dbuf[0:nb] = d0
+        w = mm(jnp.concatenate([a1, c1], axis=0), jnp.concatenate([a0, b0], axis=1))
+        cbuf[nb : 2 * nb] = w[nb:, :nb]
+        dbuf[nb : 2 * nb] = w[nb:, nb:] + d1
+        g, b = w[:nb, :nb], w[:nb, nb:] + b1
+        w = mm(c2, jnp.concatenate([g, b], axis=1))
+        cbuf[2 * nb : 3 * nb] = w[:, :nb]
+        dbuf[2 * nb : 3 * nb] = w[:, nb:] + d2
 
     def along_x(step, half):
         return remote(
@@ -295,11 +350,14 @@
                 def _():
                     along_x(step, 0).start()
 
-    third.wait_recv()
-    c2, d2 = block_map(2, g3[:, 0:part], g3[:, part : 2 * part])
-    w = mm(c2, both(ebuf))
-    cbuf[2 * nb : 3 * nb] = w[:, :nb]
-    dbuf[2 * nb : 3 * nb] = w[:, nb:] + d2
+    @pl.when(core1)
+    def _():
+        third.wait_recv()
+        packed = g3[:, 0:part]
+        c4, d4 = done(packed, middle(1, packed, g3[:, part : 2 * part]))
+        w = mm(c4, both(ebuf))
+        cbuf[2 * nb : 3 * nb] = w[:, :nb]
+        dbuf[2 * nb : 3 * nb] = w[:, nb:] + d4
 
     @pl.when(core1 & (pair == 0))
     def _():
@@ -347,15 +405,17 @@
 
     await_bytes(got1, s1.at[0])
     head.wait_send()
-    await_bytes(g2.at[pl.ds(0, rows - 1)], s2.at[0])
-    third.wait_send()
+    await_bytes(stage.at[pl.ds(0, chips - 1)], s2.at[0])
 
     @pl.when(core0)
     def _():
-        to_core1.wait_send()
+        await_bytes(stage.at[0], s2.at[0])
+        tail.wait_send()
 
     @pl.when(core1)
     def _():
+        entries.wait_send()
+        third.wait_send()
         to_pair.wait_send()
 
         @pl.when(pair == 1)
@@ -399,13 +459,13 @@
             scratch_shapes=[
                 pltpu.SMEM(offsets.shape, jnp.int32),
                 pltpu.SMEM(plan.shape, jnp.int32),
-                pltpu.VMEM((nb + 2 * own, width), F32),
+                pltpu.VMEM((3 * own, width), F32),
                 pltpu.VMEM((2, part, nb), F32),
                 pltpu.VMEM((2, part, nb), F32),
                 pltpu.VMEM((2, 2 * part, nb), F32),
                 pltpu.VMEM((cols, 2 * part, nb), F32),
-                pltpu.VMEM((rows, 4 * part, nb), F32),
-                pltpu.VMEM((rows, 4 * part, nb), F32),
+                pltpu.VMEM((rows // 2, 8 * part, nb), F32),
+                pltpu.VMEM((rows, 8 * part, nb), F32),
                 pltpu.VMEM((rows, 2 * part, nb), F32),
                 pltpu.VMEM((2,) + square, F32),
                 pltpu.VMEM((2,) + square, F32),
@@ -417,7 +477,7 @@
                 pltpu.VMEM(square, F32),
                 pltpu.VMEM((3 * nb, nb), F32),
                 pltpu.VMEM((3 * nb, width), F32),
-                dma((3,)), dma((2, 4)), dma((2,)), dma((2,)), dma((2,)), dma((2,)), dma((2,)), dma((2,)),
+                dma((3,)), dma((2, 4)), dma((4,)), dma((2,)), dma((2,)), dma((2,)), dma((2,)), dma((2,)), dma((2,)),
                 dma((rows // 4, 2)), dma((rows // 4, 2)), dma((2,)),
                 pltpu.SemaphoreType.REGULAR, pltpu.SemaphoreType.REGULAR,
                 pltpu.SemaphoreType.REGULAR,

time: 37.9 us -> 36.8 us (0.971)
  Pallas kernels: 36.4 us -> 35.3 us
    pallas_call x1, Pallas kernels: 36.4 us -> 35.3 us  [on_device(): pl.pallas_call(functools.partial(kernel, rows, cols), out_shape=pltpu.VME...]
where the time goes in v7:
time: 36.8 us; the launch traced here: 36.6 us
  Pallas kernels  35.3 us (96%)
  local copies, waits for them, and re-layouts  0.66 us (2%)
  between operations  0.66 us (2%)
    pallas_call x1, Pallas kernels, on_device(): pl.pallas_call(functools.partial(kernel, rows, cols), out_shape=pltpu.VME...  35.3 us

profile of v7, /device:TPU:7, one launch (start us, length us, event | category | flops | bytes accessed | tf_op | source)
XLA Modules:
  0.0 36.6 jit_solution(9135263982127831092)
XLA Ops:
  0.7 35.3 %chase.1 = f32[256,128]{1,0:T(8,128)S(1)} custom-call(s32[1]{0:T(128)S(6)} %copy.8.off_hbm, s32[1,30]{1,0:T(1,128)} %plan_hbm.1, f32[256,128]{1,0:T(8,128)} %e_ref.1, f32[255,1,128]{2,1,0:T(1,128)} %bitcast.1, f32[1,128,128]{2,1,0:T(8,128)} %t_ref.1), custom_call_target="tpu_custom_call" | custom-call | flops 125829120 | bytes 655360 | tf_op jit(solution)/shard_map/chase/pallas_call | solution.py:448
  35.9 0.7 %copy.7 = f32[256,128]{1,0:T(8,128)} copy(f32[256,128]{1,0:T(8,128)S(1)} %chase.1) | data formatting | bytes 262144

commit v8 on v7

--- a/solution.py
+++ b/solution.py
@@ -18,13 +18,18 @@
 
 
 def mm(a, b, rhs_t=False):
-    dims = (((1,), (1 if rhs_t else 0,)), ((), ()))
     ah, al = split(a)
     bh, bl = split(b)
     dot = functools.partial(
-        lax.dot_general, dimension_numbers=dims, preferred_element_type=F32
+        lax.dot_general,
+        dimension_numbers=(((1,), (1 if rhs_t else 0,)), ((), ())),
+        preferred_element_type=F32,
     )
-    return dot(ah, bl) + dot(al, bh) + dot(ah, bh)
+    if rhs_t:
+        return dot(ah, bl) + dot(al, bh) + dot(ah, bh)
+    return dot(ah, bl) + dot(
+        jnp.concatenate([ah, al], axis=1), jnp.concatenate([bh, bh], axis=0)
+    )
 
 
 def both(pair):
@@ -51,7 +56,7 @@
 
 def kernel(
     rows, cols, off_hbm, plan_hbm, e_ref, v_ref, t_ref, y_ref,
-    off_ref, plan_ref, xin, low, up, mine, g1, stage, g2, g3, ebuf, p1buf, fbuf, abuf, hbuf, bbuf, pbuf, sbuf, cbuf, dbuf,
+    off_ref, plan_ref, xin, xt, low, up, mine, g1, stage, g2, g3, ebuf, p1buf, fbuf, abuf, hbuf, bbuf, pbuf, sbuf, cbuf, dbuf,
     lsem, msem, hsem, s1, s2, s3, esem, psem, asem, bsend, brecv, dsem, rowsem, colsem, gosem,
 ):
     nb = t_ref.shape[1]
@@ -252,18 +257,25 @@
         lo = 2 * part * j
         return g2[:, lo : lo + part], g2[:, lo + part : lo + 2 * part]
 
-    def middle(n, packed, factor):
-        live = ((2 * r + n >= 0) & (2 * r + n < blocks)).astype(F32)
-        vectors = jnp.concatenate(triangles(packed), axis=0)
-        tv = mm(factor.reshape(nb, nb) * live, vectors, rhs_t=True)
-        return jnp.concatenate([tv[:, :nb], mm(tv[:, nb:], fresh(n))], axis=1)
-
-    def passed(n, packed, mid):
-        w = mm(triangles(packed)[1], mid)
+    def keep_transposed(blocks_of):
+        for n in blocks_of:
+            xt[n + 3] = fresh(n).T
+
+    def live(n, factor):
+        inside = ((2 * r + n >= 0) & (2 * r + n < blocks)).astype(F32)
+        return factor.reshape(nb, nb) * inside
+
+    def sides(n, lower, upper):
+        return jnp.concatenate([lower, mm(xt[n + 3], upper)], axis=0)
+
+    def passed(n, packed, factor):
+        lower, upper = triangles(packed)
+        w = mm(mm(upper, live(n, factor)), sides(n, lower, upper), rhs_t=True)
         return -w[:, :nb], fresh(n) - w[:, nb:]
 
-    def done(packed, mid):
-        w = mm(triangles(packed)[0], mid)
+    def done(n, packed, factor):
+        lower, upper = triangles(packed)
+        w = mm(mm(lower, live(n, factor)), sides(n, lower, upper), rhs_t=True)
         return eye - w[:, :nb], -w[:, nb:]
 
     entries = remote(
@@ -279,11 +291,12 @@
 
     @pl.when(core1)
     def _():
+        keep_transposed(range(-3, 2))
         await_bytes(g2.at[pl.ds(0, rows - 1)], s2.at[1])
+        third.start()
         entries.start()
-        mids = [middle(j - 3, *entry(j)) for j in range(4)]
         (a0, b0), (a1, b1), (a2, b2), (a3, b3) = [
-            passed(j - 3, entry(j)[0], mids[j]) for j in range(4)
+            passed(j - 3, *entry(j)) for j in range(4)
         ]
         first = mm(a1, jnp.concatenate([a0, b0], axis=1))
         p1buf[0] = first[:, :nb]
@@ -295,21 +308,20 @@
         fbuf[0] = w[:, :nb]
         fbuf[1] = w[:, nb:] + ebuf[1]
         to_pair.start()
-        third.start()
-        c2, d2 = done(entry(2)[0], mids[2])
+        c2, d2 = done(-1, *entry(2))
         cbuf[0:nb] = c2
         dbuf[0:nb] = d2
-        c3, d3 = done(entry(3)[0], mids[3])
+        c3, d3 = done(0, *entry(3))
         w = mm(c3, jnp.concatenate([a2, b2], axis=1))
         cbuf[nb : 2 * nb] = w[:, :nb]
         dbuf[nb : 2 * nb] = w[:, nb:] + d3
 
     @pl.when(core0)
     def _():
+        keep_transposed(range(-1, 2))
         await_bytes(g2.at[:, pl.ds(0, 6 * part)], esem.at[1])
-        mids = [middle(j - 1, *entry(j)) for j in range(3)]
-        (a0, b0), (a1, b1) = [passed(j - 1, entry(j)[0], mids[j]) for j in range(2)]
-        (c0, d0), (c1, d1), (c2, d2) = [done(entry(j)[0], mids[j]) for j in range(3)]
+        (a0, b0), (a1, b1) = [passed(j - 1, *entry(j)) for j in range(2)]
+        (c0, d0), (c1, d1), (c2, d2) = [done(j - 1, *entry(j)) for j in range(3)]
         cbuf[0:nb] = c0
         dbuf[0:nb] = d0
         w = mm(jnp.concatenate([a1, c1], axis=0), jnp.concatenate([a0, b0], axis=1))
@@ -341,7 +353,7 @@
         w = mm(late_g, early_pair)
         hbuf[0] = w[:, :nb]
         hbuf[1] = w[:, nb:] + late_b
-        for step in range(1, groups):
+        for step in range(groups - 1, 0, -1):
             @pl.when(x + step < groups)
             def _(step=step):
                 along_x(step, 1).start()
@@ -353,8 +365,7 @@
     @pl.when(core1)
     def _():
         third.wait_recv()
-        packed = g3[:, 0:part]
-        c4, d4 = done(packed, middle(1, packed, g3[:, part : 2 * part]))
+        c4, d4 = done(1, g3[:, 0:part], g3[:, part : 2 * part])
         w = mm(c4, both(ebuf))
         cbuf[2 * nb : 3 * nb] = w[:, :nb]
         dbuf[2 * nb : 3 * nb] = w[:, nb:] + d4
@@ -460,6 +471,7 @@
                 pltpu.SMEM(offsets.shape, jnp.int32),
                 pltpu.SMEM(plan.shape, jnp.int32),
                 pltpu.VMEM((3 * own, width), F32),
+                pltpu.VMEM((5, nb, width), F32),
                 pltpu.VMEM((2, part, nb), F32),
                 pltpu.VMEM((2, part, nb), F32),
                 pltpu.VMEM((2, 2 * part, nb), F32),

time: 36.8 us -> 36.5 us (level)
  no operation moved by 1% of the time
where the time goes in v8:
time: 36.5 us; the launch traced here: 36.3 us
  Pallas kernels  35 us (96%)
  local copies, waits for them, and re-layouts  0.66 us (2%)
  between operations  0.66 us (2%)
    pallas_call x1, Pallas kernels, on_device(): pl.pallas_call(functools.partial(kernel, rows, cols), out_shape=pltpu.VME...  35 us

profile of v8, /device:TPU:7, one launch (start us, length us, event | category | flops | bytes accessed | tf_op | source)
XLA Modules:
  0.0 36.3 jit_solution(13671031202372418947)
XLA Ops:
  0.7 35.0 %chase.1 = f32[256,128]{1,0:T(8,128)S(1)} custom-call(s32[1]{0:T(128)S(6)} %copy.8.off_hbm, s32[1,30]{1,0:T(1,128)} %plan_hbm.1, f32[256,128]{1,0:T(8,128)} %e_ref.1, f32[255,1,128]{2,1,0:T(1,128)} %bitcast.1, f32[1,128,128]{2,1,0:T(8,128)} %t_ref.1), custom_call_target="tpu_custom_call" | custom-call | flops 125829120 | bytes 655360 | tf_op jit(solution)/shard_map/chase/pallas_call | solution.py:459
  35.6 0.7 %copy.7 = f32[256,128]{1,0:T(8,128)} copy(f32[256,128]{1,0:T(8,128)S(1)} %chase.1) | data formatting | bytes 262144

commit v9 on v8

--- a/solution.py
+++ b/solution.py
@@ -217,20 +217,26 @@
     core0, core1 = core == 0, core == 1
     order = sorted(range(1, chips), key=lambda k: -min(k, chips - k)) + [0]
 
-    def to_chip(k):
+    def wave(h):
+        return pl.ds(4 * part * h, 4 * part)
+
+    def to_chip(k, h):
         to = 2 * lax.rem(chip + k, chips) + 1
-        return remote(stage.at[k], g2.at[r], s2.at[0], s2.at[1], to, c)
-
-    for k in order:
-        for j in range(4):
-            block = jnp.clip(4 * lax.rem(chip + k, chips) - 1 + j, 0, blocks - 1)
-            stage[k, 2 * part * j : 2 * part * (j + 1)] = g1[plan_ref[0, block]]
-    for k in order[:-1]:
-        to_chip(k).start()
-
-    @pl.when(core0)
-    def _():
-        to_chip(0).start()
+        return remote(
+            stage.at[k, wave(h)], g2.at[r, wave(h)], s2.at[0, h], s2.at[1, h], to, c
+        )
+
+    for h in range(2):
+        for k in order:
+            for j in (2 * h, 2 * h + 1):
+                block = jnp.clip(4 * lax.rem(chip + k, chips) - 1 + j, 0, blocks - 1)
+                stage[k, 2 * part * j : 2 * part * (j + 1)] = g1[plan_ref[0, block]]
+        for k in order[:-1]:
+            to_chip(k, h).start()
+
+        @pl.when(core0)
+        def _(h=h):
+            to_chip(0, h).start()
 
     @pl.when(core1)
     def _():
@@ -292,15 +298,14 @@
     @pl.when(core1)
     def _():
         keep_transposed(range(-3, 2))
-        await_bytes(g2.at[pl.ds(0, rows - 1)], s2.at[1])
+        await_bytes(g2.at[pl.ds(0, rows - 1), wave(0)], s2.at[1, 0])
         third.start()
-        entries.start()
-        (a0, b0), (a1, b1), (a2, b2), (a3, b3) = [
-            passed(j - 3, *entry(j)) for j in range(4)
-        ]
+        (a0, b0), (a1, b1) = [passed(j - 3, *entry(j)) for j in (0, 1)]
         first = mm(a1, jnp.concatenate([a0, b0], axis=1))
         p1buf[0] = first[:, :nb]
         p1buf[1] = first[:, nb:] + b1
+        await_bytes(g2.at[pl.ds(0, rows - 1), wave(1)], s2.at[1, 1])
+        (a2, b2), (a3, b3) = [passed(j - 3, *entry(j)) for j in (2, 3)]
         second = mm(a3, jnp.concatenate([a2, b2], axis=1))
         ebuf[0] = second[:, :nb]
         ebuf[1] = second[:, nb:] + b3
@@ -308,6 +313,7 @@
         fbuf[0] = w[:, :nb]
         fbuf[1] = w[:, nb:] + ebuf[1]
         to_pair.start()
+        entries.start()
         c2, d2 = done(-1, *entry(2))
         cbuf[0:nb] = c2
         dbuf[0:nb] = d2
@@ -416,11 +422,13 @@
 
     await_bytes(got1, s1.at[0])
     head.wait_send()
-    await_bytes(stage.at[pl.ds(0, chips - 1)], s2.at[0])
+    for h in range(2):
+        await_bytes(stage.at[pl.ds(0, chips - 1), wave(h)], s2.at[0, h])
 
     @pl.when(core0)
     def _():
-        await_bytes(stage.at[0], s2.at[0])
+        for h in range(2):
+            await_bytes(stage.at[0, wave(h)], s2.at[0, h])
         tail.wait_send()
 
     @pl.when(core1)
@@ -489,7 +497,7 @@
                 pltpu.VMEM(square, F32),
                 pltpu.VMEM((3 * nb, nb), F32),
                 pltpu.VMEM((3 * nb, width), F32),
-                dma((3,)), dma((2, 4)), dma((4,)), dma((2,)), dma((2,)), dma((2,)), dma((2,)), dma((2,)), dma((2,)),
+                dma((3,)), dma((2, 4)), dma((4,)), dma((2,)), dma((2, 2)), dma((2,)), dma((2,)), dma((2,)), dma((2,)),
                 dma((rows // 4, 2)), dma((rows // 4, 2)), dma((2,)),
                 pltpu.SemaphoreType.REGULAR, pltpu.SemaphoreType.REGULAR,
                 pltpu.SemaphoreType.REGULAR,

time: 36.5 us -> 36.4 us (level)
  no operation moved by 1% of the time
where the time goes in v9:
time: 36.4 us; the launch traced here: 36.2 us
  Pallas kernels  34.9 us (96%)
  local copies, waits for them, and re-layouts  0.66 us (2%)
  between operations  0.66 us (2%)
    pallas_call x1, Pallas kernels, on_device(): pl.pallas_call(functools.partial(kernel, rows, cols), out_shape=pltpu.VME...  34.9 us

profile of v9, /device:TPU:7, one launch (start us, length us, event | category | flops | bytes accessed | tf_op | source)
XLA Modules:
  0.0 36.2 jit_solution(1614181956314811563)
XLA Ops:
  0.7 34.9 %chase.1 = f32[256,128]{1,0:T(8,128)S(1)} custom-call(s32[1]{0:T(128)S(6)} %copy.8.off_hbm, s32[1,30]{1,0:T(1,128)} %plan_hbm.1, f32[256,128]{1,0:T(8,128)} %e_ref.1, f32[255,1,128]{2,1,0:T(1,128)} %bitcast.1, f32[1,128,128]{2,1,0:T(8,128)} %t_ref.1), custom_call_target="tpu_custom_call" | custom-call | flops 125829120 | bytes 655360 | tf_op jit(solution)/shard_map/chase/pallas_call | solution.py:467
  35.5 0.7 %copy.7 = f32[256,128]{1,0:T(8,128)} copy(f32[256,128]{1,0:T(8,128)S(1)} %chase.1) | data formatting | bytes 262144

commit v10 on v9

--- a/solution.py
+++ b/solution.py
@@ -396,6 +396,30 @@
         cbuf[...] = w[:, :nb]
         dbuf[...] = w[:, nb:] + dbuf[...]
 
+    gain = cbuf[pl.ds(nb - off, own)]
+    rest = dbuf[pl.ds(nb - off, own)]
+
+    await_bytes(got1, s1.at[0])
+    head.wait_send()
+    for h in range(2):
+        await_bytes(stage.at[pl.ds(0, chips - 1), wave(h)], s2.at[0, h])
+
+    @pl.when(core0)
+    def _():
+        for h in range(2):
+            await_bytes(stage.at[0, wave(h)], s2.at[0, h])
+        tail.wait_send()
+
+    @pl.when(core1)
+    def _():
+        entries.wait_send()
+        third.wait_send()
+        to_pair.wait_send()
+
+        @pl.when(pair == 1)
+        def _():
+            prefix.wait_send()
+
     @pl.when(x == 0)
     def _():
         sbuf[...] = s0
@@ -417,34 +441,14 @@
     def _():
         state.wait_recv()
 
-    dbuf[...] = mm(cbuf[...], sbuf[...]) + dbuf[...]
-    y_ref[...] = dbuf[pl.ds(nb - off, own)]
-
-    await_bytes(got1, s1.at[0])
-    head.wait_send()
-    for h in range(2):
-        await_bytes(stage.at[pl.ds(0, chips - 1), wave(h)], s2.at[0, h])
-
-    @pl.when(core0)
-    def _():
-        for h in range(2):
-            await_bytes(stage.at[0, wave(h)], s2.at[0, h])
-        tail.wait_send()
+    y_ref[...] = mm(gain, sbuf[...]) + rest
+
+    @pl.when((x > 0) & core1)
+    def _():
+        state.wait_send()
 
     @pl.when(core1)
     def _():
-        entries.wait_send()
-        third.wait_send()
-        to_pair.wait_send()
-
-        @pl.when(pair == 1)
-        def _():
-            prefix.wait_send()
-
-        @pl.when(x > 0)
-        def _():
-            state.wait_send()
-
         for step in range(1, groups):
             @pl.when(x + step < groups)
             def _(step=step):

time: 36.4 us -> 36.4 us (level)
  no operation moved by 1% of the time
where the time goes in v10:
time: 36.4 us; the launch traced here: 36.2 us
  Pallas kernels  34.9 us (96%)
  local copies, waits for them, and re-layouts  0.66 us (2%)
  between operations  0.66 us (2%)
    pallas_call x1, Pallas kernels, on_device(): pl.pallas_call(functools.partial(kernel, rows, cols), out_shape=pltpu.VME...  34.9 us

profile of v10, /device:TPU:7, one launch (start us, length us, event | category | flops | bytes accessed | tf_op | source)
XLA Modules:
  0.0 36.2 jit_solution(15984784939295028670)
XLA Ops:
  0.7 34.9 %chase.1 = f32[256,128]{1,0:T(8,128)S(1)} custom-call(s32[1]{0:T(128)S(6)} %copy.8.off_hbm, s32[1,30]{1,0:T(1,128)} %plan_hbm.1, f32[256,128]{1,0:T(8,128)} %e_ref.1, f32[255,1,128]{2,1,0:T(1,128)} %bitcast.1, f32[1,128,128]{2,1,0:T(8,128)} %t_ref.1), custom_call_target="tpu_custom_call" | custom-call | flops 125829120 | bytes 655360 | tf_op jit(solution)/shard_map/chase/pallas_call | solution.py:471
  35.5 0.7 %copy.7 = f32[256,128]{1,0:T(8,128)} copy(f32[256,128]{1,0:T(8,128)S(1)} %chase.1) | data formatting | bytes 262144

commit v11 on v9

--- a/solution.py
+++ b/solution.py
@@ -338,10 +338,10 @@
         cbuf[2 * nb : 3 * nb] = w[:, :nb]
         dbuf[2 * nb : 3 * nb] = w[:, nb:] + d2
 
-    def along_x(step, half):
+    def along_x(step, whole):
+        src, dst = (hbuf, bbuf.at[x]) if whole else (hbuf.at[1], bbuf.at[x, 1])
         return remote(
-            hbuf.at[half], bbuf.at[x, half], bsend.at[step, half], brecv.at[x, half],
-            lax.rem(r + 4 * step, rows), c,
+            src, dst, bsend.at[step, 0], brecv.at[x, 0], lax.rem(r + 4 * step, rows), c
         )
 
     @pl.when(core1)
@@ -362,11 +362,13 @@
         for step in range(groups - 1, 0, -1):
             @pl.when(x + step < groups)
             def _(step=step):
-                along_x(step, 1).start()
+                @pl.when(x == 0)
+                def _():
+                    along_x(step, False).start()
 
                 @pl.when(x > 0)
                 def _():
-                    along_x(step, 0).start()
+                    along_x(step, True).start()
 
     @pl.when(core1)
     def _():
@@ -405,9 +407,8 @@
         for source in range(groups - 1):
             @pl.when(x > source)
             def _(source=source):
-                await_bytes(bbuf.at[source, 1], brecv.at[source, 1])
+                await_bytes(bbuf.at[source] if source else bbuf.at[0, 1], brecv.at[source, 0])
                 if source:
-                    await_bytes(bbuf.at[source, 0], brecv.at[source, 0])
                     sbuf[...] = mm(bbuf[source, 0], sbuf[...]) + bbuf[source, 1]
                 else:
                     sbuf[...] = bbuf[source, 1]
@@ -448,11 +449,13 @@
         for step in range(1, groups):
             @pl.when(x + step < groups)
             def _(step=step):
-                along_x(step, 1).wait_send()
+                @pl.when(x == 0)
+                def _():
+                    along_x(step, False).wait_send()
 
                 @pl.when(x > 0)
                 def _():
-                    along_x(step, 0).wait_send()
+                    along_x(step, True).wait_send()
 
 
 def solution(mesh):

time: 36.4 us -> 36.4 us (level)
  no operation moved by 1% of the time
where the time goes in v11:
time: 36.4 us; the launch traced here: 36.2 us
  Pallas kernels  34.9 us (96%)
  local copies, waits for them, and re-layouts  0.66 us (2%)
  between operations  0.66 us (2%)
    pallas_call x1, Pallas kernels, on_device(): pl.pallas_call(functools.partial(kernel, rows, cols), out_shape=pltpu.VME...  34.9 us

profile of v11, /device:TPU:7, one launch (start us, length us, event | category | flops | bytes accessed | tf_op | source)
XLA Modules:
  0.0 36.2 jit_solution(15338932418142220047)
XLA Ops:
  0.7 34.9 %chase.1 = f32[256,128]{1,0:T(8,128)S(1)} custom-call(s32[1]{0:T(128)S(6)} %copy.8.off_hbm, s32[1,30]{1,0:T(1,128)} %plan_hbm.1, f32[256,128]{1,0:T(8,128)} %e_ref.1, f32[255,1,128]{2,1,0:T(1,128)} %bitcast.1, f32[1,128,128]{2,1,0:T(8,128)} %t_ref.1), custom_call_target="tpu_custom_call" | custom-call | flops 125829120 | bytes 655360 | tf_op jit(solution)/shard_map/chase/pallas_call | solution.py:470
  35.6 0.7 %copy.7 = f32[256,128]{1,0:T(8,128)} copy(f32[256,128]{1,0:T(8,128)S(1)} %chase.1) | data formatting | bytes 262144
